TPU v7x, 32 devices: a whole 2x2x4 slice. The times are simulated.
32 devices in a mesh: seq: 8 (over z, x), tensor: 4 (over y, core).
Axes of the slice: x: 2, y: 2, z: 4, core: 2. Of those that a mesh axis runs over, the one named last changes fastest.
Arguments:
- query_rows: bfloat16 [2048, 4096], P('seq', 'tensor'), may hold values from -5 to 5
- key_rows: bfloat16 [2048, 4096], P('seq', 'tensor'), may hold values from -5 to 5
- value_rows: bfloat16 [2048, 4096], P('seq', 'tensor'), may hold values from -6 to 6
- query_tan: bfloat16 [2048, 4096], P('seq', 'tensor'), may hold values from -6 to 6
- key_tan: bfloat16 [2048, 4096], P('seq', 'tensor'), may hold values from -6 to 6
- value_tan: bfloat16 [2048, 4096], P('seq', 'tensor'), may hold values from -6 to 6
- routes: int32 [2048, 32], P('seq', 'tensor'), may hold values from 0 to 2047, as said below
- out_weight: bfloat16 [4096, 4096], P('tensor'), may hold values from -0.125 to 0.125
Outputs:
- output: bfloat16 [2048, 4096], P('seq', 'tensor')
- output_tan: bfloat16 [2048, 4096], P('seq', 'tensor')
Inputs may be any that keep to these rules, and one draw needn't show every extreme that they name: `routes`: each head's column holds every slot of 0 to 2047 once; slot // 256 is the token's cluster. Every aligned block of 256 tokens puts exactly 32 of its tokens into each aligned block of 256 slots, for every head.
All inputs are finite; a program needn't handle non-finite values.
Results may differ from a plain program's by a relative error of at most 0.0058.
Values may be sent and summed in bfloat16 or wider, within the bound.
A program may use at most 64 MiB of HBM per device.

v0:
```python
import jax
import jax.numpy as jnp
from jax import lax
from jax.sharding import PartitionSpec as P

HEAD_SIZE = 128
CLUSTER = 256


def cluster_attend(
    query_c,
    key_c,
    value_c,
    query_cluster_gradient,
    key_cluster_gradient,
    value_cluster_gradient,
    where_pos,
):
    scaling_multiplier = HEAD_SIZE ** (-0.5)
    logit_scores = (
        jnp.einsum("cqhe,ckhe->chqk", query_c, key_c, preferred_element_type=jnp.float32)
        * scaling_multiplier
    )
    score_tangent_values = (
        jnp.einsum(
            "cqhe,ckhe->chqk", query_cluster_gradient, key_c, preferred_element_type=jnp.float32
        )
        + jnp.einsum(
            "cqhe,ckhe->chqk", query_c, key_cluster_gradient, preferred_element_type=jnp.float32
        )
    ) * scaling_multiplier
    pos_heads = jnp.transpose(where_pos, (0, 2, 1))
    visible = pos_heads[:, :, None, :] <= pos_heads[:, :, :, None]
    masked = jnp.where(visible, logit_scores, -jnp.inf)
    top_score = jnp.max(masked, axis=-1, keepdims=True)
    expo = jnp.where(visible, jnp.exp(masked - top_score), 0.0)
    attn_probs = expo / jnp.sum(expo, axis=-1, keepdims=True)
    probs_half = attn_probs.astype(jnp.bfloat16)
    attended_values = jnp.einsum(
        "chqk,ckhe->cqhe", probs_half, value_c, preferred_element_type=jnp.float32
    ).astype(jnp.bfloat16)
    tangent_probs = attn_probs * (
        score_tangent_values - jnp.sum(attn_probs * score_tangent_values, axis=-1, keepdims=True)
    )
    tangent_halfway_term = tangent_probs.astype(jnp.bfloat16)
    attended_tangent_sum = (
        jnp.einsum(
            "chqk,ckhe->cqhe", tangent_halfway_term, value_c, preferred_element_type=jnp.float32
        )
        + jnp.einsum(
            "chqk,ckhe->cqhe",
            probs_half,
            value_cluster_gradient,
            preferred_element_type=jnp.float32,
        )
    ).astype(jnp.bfloat16)
    return (attended_values, attended_tangent_sum)


def body(query_rows, key_rows, value_rows, query_tan, key_tan, value_tan, routes, out_weight):
    tok_dev = routes.shape[0]
    heads_here = routes.shape[1]
    my_index = lax.axis_index("seq")
    offset = my_index * tok_dev
    token_order = jnp.argsort(routes, axis=0)
    sorted_slots = jnp.take_along_axis(routes, token_order, axis=0)
    labels = jnp.stack([sorted_slots, token_order + offset])
    arrived = lax.all_to_all(labels, "seq", split_axis=1, concat_axis=1, tiled=True)
    recv_slot = arrived[0] - offset
    recv_pos = arrived[1]

    def by_rows(matrix):
        return jnp.take_along_axis(
            matrix.reshape(tok_dev, heads_here, HEAD_SIZE), token_order[:, :, None], axis=0
        )

    incoming = (
        lax.all_to_all(by_rows(query_rows), "seq", split_axis=0, concat_axis=0, tiled=True),
        lax.all_to_all(by_rows(key_rows), "seq", split_axis=0, concat_axis=0, tiled=True),
        lax.all_to_all(by_rows(value_rows), "seq", split_axis=0, concat_axis=0, tiled=True),
        lax.all_to_all(by_rows(query_tan), "seq", split_axis=0, concat_axis=0, tiled=True),
        lax.all_to_all(by_rows(key_tan), "seq", split_axis=0, concat_axis=0, tiled=True),
        lax.all_to_all(by_rows(value_tan), "seq", split_axis=0, concat_axis=0, tiled=True),
    )
    slot_order = jnp.argsort(recv_slot, axis=0)
    clusters = tok_dev // CLUSTER

    def to_cluster(matrix):
        placed = jnp.take_along_axis(matrix, slot_order[:, :, None], axis=0)
        return placed.reshape(clusters, CLUSTER, heads_here, HEAD_SIZE)

    cluster_pos = jnp.take_along_axis(recv_pos, slot_order, axis=0).reshape(
        clusters, CLUSTER, heads_here
    )
    attended_values, attended_tangent_sum = cluster_attend(
        *[to_cluster(matrix) for matrix in incoming], cluster_pos
    )

    def to_arrival(matrix):
        return jnp.take_along_axis(
            matrix.reshape(tok_dev, heads_here, HEAD_SIZE), recv_slot[:, :, None], axis=0
        )

    returned = (
        lax.all_to_all(to_arrival(attended_values), "seq", split_axis=0, concat_axis=0, tiled=True),
        lax.all_to_all(
            to_arrival(attended_tangent_sum), "seq", split_axis=0, concat_axis=0, tiled=True
        ),
    )
    inverse = jnp.argsort(token_order, axis=0)

    def to_tokens(matrix):
        return jnp.take_along_axis(matrix, inverse[:, :, None], axis=0).reshape(
            tok_dev, heads_here * HEAD_SIZE
        )

    head_out = to_tokens(returned[0])
    head_tan = to_tokens(returned[1])
    partial_out = jnp.dot(head_out, out_weight, preferred_element_type=jnp.float32)
    partial_tan = jnp.dot(head_tan, out_weight, preferred_element_type=jnp.float32)
    summed = (
        lax.psum_scatter(partial_out, "tensor", scatter_dimension=1, tiled=True),
        lax.psum_scatter(partial_tan, "tensor", scatter_dimension=1, tiled=True),
    )
    return (summed[0].astype(jnp.bfloat16), summed[1].astype(jnp.bfloat16))


def solution(mesh):
    return jax.shard_map(
        body,
        mesh=mesh,
        in_specs=(
            P("seq", "tensor"),
            P("seq", "tensor"),
            P("seq", "tensor"),
            P("seq", "tensor"),
            P("seq", "tensor"),
            P("seq", "tensor"),
            P("seq", "tensor"),
            P("tensor", None),
        ),
        out_specs=(P("seq", "tensor"), P("seq", "tensor")),
        check_vma=False,
    )
```

profile of v0, /device:TPU:16, one launch (start us, length us, event | category | flops | bytes accessed | tf_op | source)
XLA Modules:
  0.0 476.1 jit_solution(17698170225785063899)
XLA Ops:
  7.2 4.0 sort.45
  11.5 13.0 %gather_fusion.1 = s32[2048]{0:T(1024)S(1)} fusion(s32[256,8]{0,1:T(8,128)S(1)} %copy-done, s32[2048]{0:T(1024)S(1)} %reshape.269), kind=kCustom, calls=%fused_computation.1.clone | custom fusion | bytes 32768 | tf_op jit(solution)/shard_map/jit(take_along_axis)/gather | solution.py:66
  24.8 1.0 reshape.338
  25.8 6.1 %all-to-all-start.1 = ((s32[8,1,512]{2,1,0:T(1,128)}), s32[8,1,512]{2,1,0:T(1,128)S(1)}, u32[]{:S(2)}, u32[]{:S(2)}) async-start(s32[8,1,512]{2,1,0:T(1,128)} %reshape.338), calls=%async_computation.1 | async-start | bytes 32768 | tf_op jit(solution)/shard_map/all_to_all | solution.py:68
  32.6 10.1 %gather_fusion.4 = bf16[2048,128]{1,0:T(8,128)(2,1)S(1)} fusion(bf16[256,8,128]{2,1,0:T(8,128)(2,1)S(1)} %bitcast.139, s32[2048]{0:T(1024)S(1)} %reshape.264), kind=kCustom, calls=%fused_computation.3.clone | custom fusion | bytes 1064960 | tf_op jit(solution)/shard_map/jit(take_along_axis)/gather | solution.py:73
  42.7 10.1 %gather_fusion.6 = bf16[2048,128]{1,0:T(8,128)(2,1)S(1)} fusion(bf16[256,8,128]{2,1,0:T(8,128)(2,1)S(1)} %bitcast.138, s32[2048]{0:T(1024)S(1)} %reshape.264), kind=kCustom, calls=%fused_computation.5.clone | custom fusion | bytes 1064960 | tf_op jit(solution)/shard_map/jit(take_along_axis)/gather | solution.py:73
  52.9 10.1 %gather_fusion = bf16[2048,128]{1,0:T(8,128)(2,1)S(1)} fusion(bf16[256,8,128]{2,1,0:T(8,128)(2,1)S(1)} %bitcast.141, s32[2048]{0:T(1024)S(1)} %reshape.264), kind=kCustom, calls=%fused_computation.clone | custom fusion | bytes 1064960 | tf_op jit(solution)/shard_map/jit(take_along_axis)/gather | solution.py:73
  63.1 19.5 %gather_fusion.10 = bf16[2048,128]{1,0:T(8,128)(2,1)} fusion(bf16[256,8,128]{2,1,0:T(8,128)(2,1)S(1)} %bitcast.142, s32[2048]{0:T(1024)S(1)} %reshape.264), kind=kCustom, calls=%fused_computation.9.clone | custom fusion | bytes 1064960 | tf_op jit(solution)/shard_map/jit(take_along_axis)/gather | solution.py:73
  82.8 19.3 %gather_fusion.12 = bf16[2048,128]{1,0:T(8,128)(2,1)} fusion(bf16[256,8,128]{2,1,0:T(8,128)(2,1)S(1)} %bitcast.143, s32[2048]{0:T(1024)S(1)} %reshape.264), kind=kCustom, calls=%fused_computation.11.clone | custom fusion | bytes 1064960 | tf_op jit(solution)/shard_map/jit(take_along_axis)/gather | solution.py:73
  102.2 19.5 %gather_fusion.14 = bf16[2048,128]{1,0:T(8,128)(2,1)} fusion(bf16[256,8,128]{2,1,0:T(8,128)(2,1)S(1)} %bitcast.140, s32[2048]{0:T(1024)S(1)} %reshape.264), kind=kCustom, calls=%fused_computation.13.clone | custom fusion | bytes 1064960 | tf_op jit(solution)/shard_map/jit(take_along_axis)/gather | solution.py:73
  121.7 2.5 bitcast_select_fusion.2
  124.2 17.9 %all_to_all.45 = bf16[256,8,128]{2,1,0:T(8,128)(2,1)S(1)} all-to-all(bf16[256,8,128]{2,1,0:T(8,128)(2,1)S(1)} %get-tuple-element.16), channel_id=1, replica_groups=mesh['seq'=8,'tensor'=4] {'seq'}, dimensions={0} | all-to-all | bytes 1048576 | tf_op jit(solution)/shard_map/all_to_all | solution.py:83
  142.1 17.4 %all_to_all.46 = bf16[256,8,128]{2,1,0:T(8,128)(2,1)S(1)} all-to-all(bf16[256,8,128]{2,1,0:T(8,128)(2,1)S(1)} %get-tuple-element.17), channel_id=1, replica_groups=mesh['seq'=8,'tensor'=4] {'seq'}, dimensions={0} | all-to-all | bytes 1048576 | tf_op jit(solution)/shard_map/all_to_all | solution.py:78
  159.5 17.4 %all_to_all.47 = bf16[256,8,128]{2,1,0:T(8,128)(2,1)S(1)} all-to-all(bf16[256,8,128]{2,1,0:T(8,128)(2,1)S(1)} %get-tuple-element.18), channel_id=1, replica_groups=mesh['seq'=8,'tensor'=4] {'seq'}, dimensions={0} | all-to-all | bytes 1048576 | tf_op jit(solution)/shard_map/all_to_all | solution.py:79
  177.0 5.4 %all-to-all-start = ((bf16[256,8,128]{2,1,0:T(8,128)(2,1)}), bf16[256,8,128]{2,1,0:T(8,128)(2,1)S(1)}, u32[]{:S(2)}, u32[]{:S(2)}) async-start(bf16[256,8,128]{2,1,0:T(8,128)(2,1)} %get-tuple-element.21), calls=%async_computation | async-start | bytes 1048576 | tf_op jit(solution)/shard_map/all_to_all | solution.py:80
  182.4 0.5 broadcast.454
  182.9 0.7 reduce.6
  184.3 9.8 %all-to-all-done = bf16[256,8,128]{2,1,0:T(8,128)(2,1)S(1)} async-done(((bf16[256,8,128]{2,1,0:T(8,128)(2,1)}), bf16[256,8,128]{2,1,0:T(8,128)(2,1)S(1)}, u32[]{:S(2)}, u32[]{:S(2)}) %all-to-all-start) | async-done | bytes 524320 | tf_op jit(solution)/shard_map/all_to_all | solution.py:80
  194.1 6.0 %all-to-all-start.5 = ((bf16[256,8,128]{2,1,0:T(8,128)(2,1)}), bf16[256,8,128]{2,1,0:T(8,128)(2,1)S(1)}, u32[]{:S(2)}, u32[]{:S(2)}) async-start(bf16[256,8,128]{2,1,0:T(8,128)(2,1)} %get-tuple-element.19), calls=%async_computation.6 | async-start | bytes 1048576 | tf_op jit(solution)/shard_map/all_to_all | solution.py:81
  200.3 3.3 sort.46
  203.8 14.1 %gather_fusion.3 = s32[2048]{0:T(1024)S(1)} fusion(s32[256,8]{1,0:T(8,128)S(1)} %bitcast.137, s32[2048]{0:T(1024)S(1)} %reshape.278), kind=kCustom, calls=%fused_computation.17.clone | custom fusion | bytes 32768 | tf_op jit(solution)/shard_map/jit(take_along_axis)/gather | solution.py:92
  218.6 10.1 %gather_fusion.15 = bf16[2048,128]{1,0:T(8,128)(2,1)S(1)} fusion(bf16[256,8,128]{2,1,0:T(8,128)(2,1)S(1)} %all_to_all.45, s32[2048]{0:T(1024)S(1)} %reshape.273), kind=kCustom, calls=%fused_computation.14.clone | custom fusion | bytes 1064960 | tf_op jit(solution)/shard_map/jit(take_along_axis)/gather | solution.py:89
  228.6 1.1 copy.102
  229.8 10.1 %gather_fusion.2 = bf16[2048,128]{1,0:T(8,128)(2,1)S(1)} fusion(bf16[256,8,128]{2,1,0:T(8,128)(2,1)S(1)} %all-to-all-done, s32[2048]{0:T(1024)S(1)} %reshape.273), kind=kCustom, calls=%fused_computation.2.clone | custom fusion | bytes 1064960 | tf_op jit(solution)/shard_map/jit(take_along_axis)/gather | solution.py:89
  240.2 10.1 %gather_fusion.5 = bf16[2048,128]{1,0:T(8,128)(2,1)S(1)} fusion(bf16[256,8,128]{2,1,0:T(8,128)(2,1)S(1)} %all_to_all.46, s32[2048]{0:T(1024)S(1)} %reshape.273), kind=kCustom, calls=%fused_computation.4.clone | custom fusion | bytes 1064960 | tf_op jit(solution)/shard_map/jit(take_along_axis)/gather | solution.py:89
  250.3 10.1 %gather_fusion.7 = bf16[2048,128]{1,0:T(8,128)(2,1)S(1)} fusion(bf16[256,8,128]{2,1,0:T(8,128)(2,1)S(1)} %all_to_all.47, s32[2048]{0:T(1024)S(1)} %reshape.273), kind=kCustom, calls=%fused_computation.6.clone | custom fusion | bytes 1064960 | tf_op jit(solution)/shard_map/jit(take_along_axis)/gather | solution.py:89
  260.4 6.0 %all-to-all-start.6 = ((bf16[256,8,128]{2,1,0:T(8,128)(2,1)}), bf16[256,8,128]{2,1,0:T(8,128)(2,1)S(1)}, u32[]{:S(2)}, u32[]{:S(2)}) async-start(bf16[256,8,128]{2,1,0:T(8,128)(2,1)} %get-tuple-element.20), calls=%async_computation.7 | async-start | bytes 1048576 | tf_op jit(solution)/shard_map/all_to_all | solution.py:82
  266.4 3.1 fusion.43
  269.4 1.9 fusion.3
  271.7 10.1 %gather_fusion.11 = bf16[2048,128]{1,0:T(8,128)(2,1)S(1)} fusion(bf16[256,8,128]{2,1,0:T(8,128)(2,1)S(1)} %all-to-all-done.5, s32[2048]{0:T(1024)S(1)} %reshape.273), kind=kCustom, calls=%fused_computation.10.clone | custom fusion | bytes 1064960 | tf_op jit(solution)/shard_map/jit(take_along_axis)/gather | solution.py:89
  281.8 2.0 fusion.17
  283.8 10.1 %gather_fusion.13 = bf16[2048,128]{1,0:T(8,128)(2,1)S(1)} fusion(bf16[256,8,128]{2,1,0:T(8,128)(2,1)S(1)} %all-to-all-done.6, s32[2048]{0:T(1024)S(1)} %reshape.273), kind=kCustom, calls=%fused_computation.12.clone | custom fusion | bytes 1064960 | tf_op jit(solution)/shard_map/jit(take_along_axis)/gather | solution.py:89
  293.9 2.9 multiply_reduce_fusion
  297.3 0.6 copy-done.7
  298.5 10.1 %gather_fusion.8 = bf16[2048,128]{1,0:T(8,128)(2,1)S(1)} fusion(bf16[256,8,128]{2,1,0:T(8,128)(2,1)S(1)} %copy.86, s32[2048]{0:T(1024)S(1)} %reshape.298), kind=kCustom, calls=%fused_computation.7.clone | custom fusion | bytes 1064960 | tf_op jit(solution)/shard_map/jit(take_along_axis)/gather | solution.py:100
  308.6 10.1 %gather_fusion.16 = bf16[2048,128]{1,0:T(8,128)(2,1)S(1)} fusion(bf16[256,8,128]{2,1,0:T(8,128)(2,1)S(1)} %copy.105, s32[2048]{0:T(1024)S(1)} %reshape.298), kind=kCustom, calls=%fused_computation.15.clone | custom fusion | bytes 1064960 | tf_op jit(solution)/shard_map/jit(take_along_axis)/gather | solution.py:100
  318.6 1.1 bitcast_select_fusion.1
  319.8 17.1 %all_to_all.48 = bf16[256,8,128]{2,1,0:T(8,128)(2,1)S(1)} all-to-all(bf16[256,8,128]{2,1,0:T(8,128)(2,1)S(1)} %get-tuple-element.14), channel_id=1, replica_groups=mesh['seq'=8,'tensor'=4] {'seq'}, dimensions={0} | all-to-all | bytes 1048576 | tf_op jit(solution)/shard_map/all_to_all | solution.py:106
  336.9 5.4 %all-to-all-start.4 = ((bf16[256,8,128]{2,1,0:T(8,128)(2,1)}), bf16[256,8,128]{2,1,0:T(8,128)(2,1)S(1)}, u32[]{:S(2)}, u32[]{:S(2)}) async-start(bf16[256,8,128]{2,1,0:T(8,128)(2,1)} %get-tuple-element.15), calls=%async_computation.4 | async-start | bytes 1048576 | tf_op jit(solution)/shard_map/all_to_all | solution.py:105
  342.3 3.3 sort.47
  346.0 10.1 %gather_fusion.17 = bf16[2048,128]{1,0:T(8,128)(2,1)S(1)} fusion(bf16[256,8,128]{2,1,0:T(8,128)(2,1)S(1)} %all_to_all.48, s32[2048]{0:T(1024)S(1)} %reshape.302), kind=kCustom, calls=%fused_computation.16.clone | custom fusion | bytes 1064960 | tf_op jit(solution)/shard_map/jit(take_along_axis)/gather | solution.py:113
  356.1 10.1 %gather_fusion.9 = bf16[2048,128]{1,0:T(8,128)(2,1)S(1)} fusion(bf16[256,8,128]{2,1,0:T(8,128)(2,1)S(1)} %all-to-all-done.4, s32[2048]{0:T(1024)S(1)} %reshape.302), kind=kCustom, calls=%fused_computation.8.clone | custom fusion | bytes 1064960 | tf_op jit(solution)/shard_map/jit(take_along_axis)/gather | solution.py:113
  366.7 7.6 %fusion.14 = f32[256,4096]{1,0:T(8,128)} fusion(bf16[1024,4096]{1,0:T(8,128)(2,1)} %param.19, bf16[32,8,8,128]{3,2,1,0:T(8,128)(2,1)S(1)} %bitcast.145), kind=kOutput, calls=%fused_computation.40 | convolution fusion | flops 2147483648 | bytes 13107200 | tf_op jit(solution)/shard_map/dot_general | solution.py:119
  374.4 7.8 %fusion.11 = f32[256,4096]{1,0:T(8,128)} fusion(bf16[1024,4096]{1,0:T(8,128)(2,1)} %param.19, bf16[32,8,8,128]{3,2,1,0:T(8,128)(2,1)S(1)} %bitcast.144), kind=kOutput, calls=%fused_computation.37 | convolution fusion | flops 2147483648 | bytes 13107200 | tf_op jit(solution)/shard_map/dot_general | solution.py:120
  382.2 37.8 %reduce-scatter.3.cloned.1.call-done = f32[256,1024]{1,0:T(8,128)} async-done(((f32[256,4096]{1,0:T(8,128)}), f32[256,1024]{1,0:T(8,128)}) %reduce-scatter.3.cloned.1.call-update) | async-done | bytes 1048592 | tf_op jit(solution)/shard_map/reduce_scatter | solution.py:122
  420.0 2.1 convert_element_type.36
  422.1 45.1 %reduce-scatter.5.cloned.1.call-done = f32[256,1024]{1,0:T(8,128)} async-done(((f32[256,4096]{1,0:T(8,128)}), f32[256,1024]{1,0:T(8,128)}) %reduce-scatter.5.cloned.1.call-update) | async-done | bytes 1048592 | tf_op jit(solution)/shard_map/reduce_scatter | solution.py:123
  467.2 2.1 convert_element_type.41
  (79 shorter events, 6.1 us)
Async XLA Ops:
  7.2 4.3 copy-start
  11.5 20.9 %copy-start.1 = (bf16[256,1024]{1,0:T(8,128)(2,1)S(1)}, bf16[256,1024]{1,0:T(8,128)(2,1)}, u32[]{:S(2)}) copy-start(bf16[256,1024]{1,0:T(8,128)(2,1)} %param.12) | copy-start | bytes 1572868
  24.5 8.0 %copy-start.2 = (bf16[256,1024]{1,0:T(8,128)(2,1)S(1)}, bf16[256,1024]{1,0:T(8,128)(2,1)}, u32[]{:S(2)}) copy-start(bf16[256,1024]{1,0:T(8,128)(2,1)} %param.13) | copy-start | bytes 1572868
  25.8 98.4 %all-to-all-start.1 = ((s32[8,1,512]{2,1,0:T(1,128)}), s32[8,1,512]{2,1,0:T(1,128)S(1)}, u32[]{:S(2)}, u32[]{:S(2)}) async-start(s32[8,1,512]{2,1,0:T(1,128)} %reshape.338), calls=%async_computation.1 | async-start | bytes 32768 | tf_op jit(solution)/shard_map/all_to_all | solution.py:68
  42.7 10.1 %copy-start.3 = (bf16[256,1024]{1,0:T(8,128)(2,1)S(1)}, bf16[256,1024]{1,0:T(8,128)(2,1)}, u32[]{:S(2)}) copy-start(bf16[256,1024]{1,0:T(8,128)(2,1)} %param.14) | copy-start | bytes 1572868
  52.9 10.1 %copy-start.4 = (bf16[256,1024]{1,0:T(8,128)(2,1)S(1)}, bf16[256,1024]{1,0:T(8,128)(2,1)}, u32[]{:S(2)}) copy-start(bf16[256,1024]{1,0:T(8,128)(2,1)} %param.15) | copy-start | bytes 1572868
  63.1 19.5 %copy-start.5 = (bf16[256,1024]{1,0:T(8,128)(2,1)S(1)}, bf16[256,1024]{1,0:T(8,128)(2,1)}, u32[]{:S(2)}) copy-start(bf16[256,1024]{1,0:T(8,128)(2,1)} %param.16) | copy-start | bytes 1572868
  82.7 19.3 %copy-start.6 = (bf16[256,1024]{1,0:T(8,128)(2,1)S(1)}, bf16[256,1024]{1,0:T(8,128)(2,1)}, u32[]{:S(2)}) copy-start(bf16[256,1024]{1,0:T(8,128)(2,1)} %param.17) | copy-start | bytes 1572868
  177.0 17.1 %all-to-all-start = ((bf16[256,8,128]{2,1,0:T(8,128)(2,1)}), bf16[256,8,128]{2,1,0:T(8,128)(2,1)S(1)}, u32[]{:S(2)}, u32[]{:S(2)}) async-start(bf16[256,8,128]{2,1,0:T(8,128)(2,1)} %get-tuple-element.21), calls=%async_computation | async-start | bytes 1048576 | tf_op jit(solution)/shard_map/all_to_all | solution.py:80
  194.1 66.2 %all-to-all-start.5 = ((bf16[256,8,128]{2,1,0:T(8,128)(2,1)}), bf16[256,8,128]{2,1,0:T(8,128)(2,1)S(1)}, u32[]{:S(2)}, u32[]{:S(2)}) async-start(bf16[256,8,128]{2,1,0:T(8,128)(2,1)} %get-tuple-element.19), calls=%async_computation.6 | async-start | bytes 1048576 | tf_op jit(solution)/shard_map/all_to_all | solution.py:81
  250.3 16.1 %copy-start.8 = (bf16[2048,128]{1,0:T(8,128)(2,1)}, bf16[2048,128]{1,0:T(8,128)(2,1)S(1)}, u32[]{:S(2)}) copy-start(bf16[2048,128]{1,0:T(8,128)(2,1)S(1)} %gather_fusion.5) | copy-start | bytes 1572868
  260.4 23.4 %all-to-all-start.6 = ((bf16[256,8,128]{2,1,0:T(8,128)(2,1)}), bf16[256,8,128]{2,1,0:T(8,128)(2,1)S(1)}, u32[]{:S(2)}, u32[]{:S(2)}) async-start(bf16[256,8,128]{2,1,0:T(8,128)(2,1)} %get-tuple-element.20), calls=%async_computation.7 | async-start | bytes 1048576 | tf_op jit(solution)/shard_map/all_to_all | solution.py:82
  283.8 10.1 %copy-start.9 = (bf16[2048,128]{1,0:T(8,128)(2,1)S(1)}, bf16[2048,128]{1,0:T(8,128)(2,1)}, u32[]{:S(2)}) copy-start(bf16[2048,128]{1,0:T(8,128)(2,1)} %copy-done.8) | copy-start | bytes 1572868
  293.9 2.9 copy-start.10
  296.8 1.0 copy-start.7
  336.9 19.2 %all-to-all-start.4 = ((bf16[256,8,128]{2,1,0:T(8,128)(2,1)}), bf16[256,8,128]{2,1,0:T(8,128)(2,1)S(1)}, u32[]{:S(2)}, u32[]{:S(2)}) async-start(bf16[256,8,128]{2,1,0:T(8,128)(2,1)} %get-tuple-element.15), calls=%async_computation.4 | async-start | bytes 1048576 | tf_op jit(solution)/shard_map/all_to_all | solution.py:105
  342.3 77.6 %reduce-scatter.3.cloned.1.call-start = ((), (), s32[]{:S(2)}) async-start(), calls=%async_computation.11 | async-start | bytes 5242880 | tf_op jit(solution)/shard_map/reduce_scatter | solution.py:122
  374.3 92.9 %reduce-scatter.5.cloned.1.call-start = ((), (), s32[]{:S(2)}) async-start(), calls=%async_computation.12 | async-start | bytes 5242880 | tf_op jit(solution)/shard_map/reduce_scatter | solution.py:123
Sparse Core Ops, SparseCore 0:
  374.5 45.4 reduce-scatter.2
  422.7 44.5 reduce-scatter.4
where the time goes:
time: 479 us; the launch traced here: 476 us
  local copies, waits for them, and re-layouts  224 us (47%)
  waiting for transfers between devices  92.7 us (19%)
  blocking collectives  69.8 us (15%)
  starting transfers between devices  29.1 us (6%)
  matrix products  26.1 us (5%)
  other arithmetic  19.6 us (4%)
  between operations  14.6 us (3%)
    gather x8, local copies, waits for them, and re-layouts, by_rows(): jnp.take_along_axis(matrix.reshape(tok_dev, heads_here, HEAD_SIZE), token...  88.8 us
    gather x10, local copies, waits for them, and re-layouts, to_cluster(): placed = jnp.take_along_axis(matrix, slot_order[:, :, None], axis=0)  62.1 us
    reduce_scatter x1, waiting for transfers between devices, body(): lax.psum_scatter(partial_tan, 'tensor', scatter_dimension=1, tiled=True)  45.1 us
    reduce_scatter x1, waiting for transfers between devices, body(): lax.psum_scatter(partial_out, 'tensor', scatter_dimension=1, tiled=True)  37.8 us
    gather x4, local copies, waits for them, and re-layouts, to_arrival(): jnp.take_along_axis(matrix.reshape(tok_dev, heads_here, HEAD_SIZE), recv_...  20.4 us
    gather x4, local copies, waits for them, and re-layouts, to_tokens(): jnp.take_along_axis(matrix, inverse[:, :, None], axis=0)  20.4 us
    all_to_all x1, blocking collectives, body(): lax.all_to_all(by_rows(value_tan), 'seq', split_axis=0, concat_axis=0, ti...  17.9 us
    all_to_all x1, blocking collectives, body(): lax.all_to_all(by_rows(query_rows), 'seq', split_axis=0, concat_axis=0, t...  17.4 us
  transfers between devices with their start and end apart: 7, of which 3 were waited for; matrix products, arithmetic and copies ran while one was open for 41% of the time, Pallas kernels for 0%

commit v1 on v0

v1 whole, which is shorter than its diff:
```python
import jax
import jax.numpy as jnp
from jax import lax
from jax.sharding import PartitionSpec as P

HEAD_SIZE = 128


def body(n, query_rows, key_rows, value_rows, query_tan, key_tan, value_tan, routes, out_weight):
    tok_dev, heads = routes.shape
    per = tok_dev // n
    member = (routes // tok_dev)[:, :, None] == jnp.arange(n)
    earlier = jnp.tril(jnp.ones((tok_dev, tok_dev), jnp.bfloat16), -1)
    rank = jnp.einsum(
        "ts,shc->thc", earlier, member.astype(jnp.bfloat16), preferred_element_type=jnp.float32
    )
    place = jnp.sum(jnp.where(member, rank + per * jnp.arange(n, dtype=jnp.float32), 0.0), -1)
    order = (place[:, :, None] == jnp.arange(tok_dev, dtype=jnp.float32)).astype(jnp.bfloat16)
    order = jnp.transpose(order, (1, 0, 2))
    rows = jnp.concatenate(
        [
            m.reshape(tok_dev, heads, HEAD_SIZE)
            for m in (query_tan, query_rows, key_rows, key_tan, value_rows, value_tan)
        ],
        -1,
    )
    sent = jnp.einsum("htp,the->phe", order, rows, preferred_element_type=jnp.float32)
    got = lax.all_to_all(
        sent.astype(jnp.bfloat16), "seq", split_axis=0, concat_axis=0, tiled=True
    )
    e = HEAD_SIZE
    query, key = got[:, :, e : 2 * e], got[:, :, 2 * e : 3 * e]
    value, values = got[:, :, 4 * e : 5 * e], got[:, :, 4 * e :]
    scale = HEAD_SIZE**-0.5
    scores = jnp.einsum("qhe,khe->hqk", query, key, preferred_element_type=jnp.float32) * scale
    tangent = (
        jnp.einsum(
            "qhe,khe->hqk",
            got[:, :, : 2 * e],
            got[:, :, 2 * e : 4 * e],
            preferred_element_type=jnp.float32,
        )
        * scale
    )
    visible = jnp.tril(jnp.ones((tok_dev, tok_dev), bool))
    masked = jnp.where(visible, scores, -jnp.inf)
    expo = jnp.exp(masked - jnp.max(masked, -1, keepdims=True))
    probs = expo / jnp.sum(expo, -1, keepdims=True)
    tangent_probs = probs * (tangent - jnp.sum(probs * tangent, -1, keepdims=True))
    both = jnp.einsum(
        "hqk,khe->qhe", probs.astype(jnp.bfloat16), values, preferred_element_type=jnp.float32
    )
    extra = jnp.einsum(
        "hqk,khe->qhe", tangent_probs.astype(jnp.bfloat16), value, preferred_element_type=jnp.float32
    )
    result = jnp.concatenate([both[:, :, :e], both[:, :, e:] + extra], -1).astype(jnp.bfloat16)
    back = lax.all_to_all(result, "seq", split_axis=0, concat_axis=0, tiled=True)
    home = jnp.einsum("htp,phe->the", order, back, preferred_element_type=jnp.float32)
    home = home.astype(jnp.bfloat16)
    stacked = jnp.concatenate(
        [home[:, :, :e].reshape(tok_dev, -1), home[:, :, e:].reshape(tok_dev, -1)], 0
    )
    partial = jnp.dot(stacked, out_weight, preferred_element_type=jnp.float32)
    total = lax.psum_scatter(
        partial.astype(jnp.bfloat16), "tensor", scatter_dimension=1, tiled=True
    )
    return (total[:tok_dev], total[tok_dev:])


def solution(mesh):
    n = mesh.shape["seq"]
    return jax.shard_map(
        lambda *args: body(n, *args),
        mesh=mesh,
        in_specs=(P("seq", "tensor"),) * 7 + (P("tensor", None),),
        out_specs=(P("seq", "tensor"), P("seq", "tensor")),
        check_vma=False,
    )
```

time: 479 us -> 205 us (0.43)
  local copies, waits for them, and re-layouts: 224 us -> 19.2 us
  blocking collectives: 69.8 us -> 30.8 us
  starting transfers between devices: 29.1 us -> 6.14 us
  waiting for transfers between devices: 92.7 us -> 112 us
  other arithmetic: 19.6 us -> 0.9 us
  matrix products: 26.1 us -> 18.9 us
    gather x36 -> x0, local copies, waits for them, and re-layouts: 220 us -> none  [the longest x8 88.8 us: by_rows(): jnp.take_along_axis(matrix.reshape(tok_dev, heads_here, HEAD_SIZE), token...]
    all_to_all x5 -> x1, waiting for transfers between devices: 9.79 us -> 67.4 us  [body(): lax.all_to_all(sent.astype(jnp.bfloat16), 'seq', split_axis=0, concat_axi...]
    all_to_all x4 -> x1, blocking collectives: 69.8 us -> 30.8 us  [body(): lax.all_to_all(result, 'seq', split_axis=0, concat_axis=0, tiled=True)]
    reduce_scatter x2 -> x1, waiting for transfers between devices: 82.9 us -> 45.1 us  [body(): lax.psum_scatter(partial.astype(jnp.bfloat16), 'tensor', scatter_dimensio...]
    all_to_all x5 -> x1, starting transfers between devices: 29 us -> 6.14 us  [body(): lax.all_to_all(sent.astype(jnp.bfloat16), 'seq', split_axis=0, concat_axi...]
    sort x3 -> x0, other arithmetic: 10.5 us -> none  [the longest x1 4 us: body(): token_order = jnp.argsort(routes, axis=0)]
    dot_general x7 -> x6, matrix products: 23.1 us -> 15.3 us  [the longest x1 9.63 us: body(): partial = jnp.dot(stacked, out_weight, preferred_element_type=jnp.float32)]
    unnamed x31 -> x23, local copies, waits for them, and re-layouts: 2.66 us -> 9.82 us
  transfers between devices with their start and end apart: 7 -> 2, of which waited for: 3 -> 2; matrix products, arithmetic and copies ran while one was open for 41% -> 0% of each run, Pallas kernels for 0% -> 0%
where the time goes in v1:
time: 205 us; the launch traced here: 203 us
  waiting for transfers between devices  112 us (55%)
  blocking collectives  30.8 us (15%)
  local copies, waits for them, and re-layouts  19.2 us (9%)
  matrix products  18.9 us (9%)
  between operations  14.2 us (7%)
  starting transfers between devices  6.14 us (3%)
    all_to_all x1, waiting for transfers between devices, body(): lax.all_to_all(sent.astype(jnp.bfloat16), 'seq', split_axis=0, concat_axi...  67.4 us
    reduce_scatter x1, waiting for transfers between devices, body(): lax.psum_scatter(partial.astype(jnp.bfloat16), 'tensor', scatter_dimensio...  45.1 us
    all_to_all x1, blocking collectives, body(): lax.all_to_all(result, 'seq', split_axis=0, concat_axis=0, tiled=True)  30.8 us
    unnamed x23, local copies, waits for them, and re-layouts  9.82 us
    dot_general x1, matrix products, body(): partial = jnp.dot(stacked, out_weight, preferred_element_type=jnp.float32)  9.63 us
    all_to_all x1, starting transfers between devices, body(): lax.all_to_all(sent.astype(jnp.bfloat16), 'seq', split_axis=0, concat_axi...  6.14 us
  transfers between devices with their start and end apart: 2, of which 2 were waited for; matrix products, arithmetic and copies ran while one was open for 0% of the time, Pallas kernels for 0%

profile of v1, /device:TPU:16, one launch (start us, length us, event | category | flops | bytes accessed | tf_op | source)
XLA Modules:
  0.0 202.6 jit_solution(6556570989994292093)
XLA Ops:
  7.2 0.0 copy-start
  7.2 0.0 copy-start.1
  7.2 0.8 add_select_fusion
  8.0 0.0 copy-start.2
  8.0 1.3 copy.21
  9.3 0.8 constant_dynamic-update-slice_fusion.5
  10.2 0.0 copy-done
  10.2 0.0 copy-start.3
  10.2 0.2 copy.22
  10.4 0.0 copy-done.1
  10.4 0.2 copy.23
  10.6 0.0 copy-done.2
  10.6 0.2 copy.24
  10.8 0.4 copy-done.3
  11.2 0.2 copy.25
  11.4 1.2 copy.26
  12.7 0.8 constant_dynamic-update-slice_fusion.4
  13.5 0.9 constant_dynamic-update-slice_fusion.3
  14.4 0.9 constant_dynamic-update-slice_fusion.2
  15.2 0.9 constant_dynamic-update-slice_fusion.1
  16.1 0.9 constant_dynamic-update-slice_fusion
  17.0 0.3 fusion.9
  17.2 3.0 %convert_bitcast_fusion = bf16[256,8,768]{0,2,1:T(8,128)(2,1)S(1)} fusion(bf16[256,8,768]{0,2,1:T(8,128)(2,1)} %constant_dynamic-update-slice_fusion, f32[8,256]{1,0:T(8,128)S(1)} %bitcast.42), kind=kOutput, calls=%fused_computation.2 | convolution fusion | flops 807403520 | bytes 6299648 | tf_op jit(solution)/shard_map/htp,the->phe/dot_general | solution.py:27
  20.2 3.7 %copy.27 = bf16[256,8,768]{2,1,0:T(8,128)(2,1)} copy(bf16[256,8,768]{0,2,1:T(8,128)(2,1)S(1)} %convert_bitcast_fusion) | data formatting | bytes 6291456 | tf_op jit(solution)/shard_map/convert_element_type | solution.py:29
  23.9 6.1 %all-to-all-start = ((bf16[256,8,768]{2,1,0:T(8,128)(2,1)}), bf16[256,8,768]{2,1,0:T(8,128)(2,1)S(1)}, u32[]{:S(2)}, u32[]{:S(2)}) async-start(bf16[256,8,768]{2,1,0:T(8,128)(2,1)} %copy.27), calls=%async_computation | async-start | bytes 6291456 | tf_op jit(solution)/shard_map/all_to_all | solution.py:28
  30.1 0.0 reduce-scatter.2.cloned.1.call-start
  30.1 67.4 %all-to-all-done = bf16[256,8,768]{2,1,0:T(8,128)(2,1)S(1)} async-done(((bf16[256,8,768]{2,1,0:T(8,128)(2,1)}), bf16[256,8,768]{2,1,0:T(8,128)(2,1)S(1)}, u32[]{:S(2)}, u32[]{:S(2)}) %all-to-all-start) | async-done | bytes 3145760 | tf_op jit(solution)/shard_map/all_to_all | solution.py:28
  97.5 1.2 fusion.58
  98.7 3.3 %fusion.62 = (f32[8,256]{1,0:T(8,128)S(1)}, f32[8,256,256]{1,2,0:T(8,128)}) fusion(pred[256,256]{0,1:T(8,128)(4,1)S(1)} %iota_compare_fusion.7, bf16[256,8,128]{2,1,0:T(8,128)(2,1)} %get-tuple-element.3, bf16[256,8,128]{2,1,0:T(8,128)(2,1)} %get-tuple-element.4), kind=kOutput, calls=%fused_computation.77 | convolution fusion | flops 136315136 | bytes 3219456 | tf_op jit(solution)/shard_map/sub | solution.py:47
  102.1 0.0 copy-start.5
  102.1 0.2 fusion.59
  102.3 1.4 copy-done.5
  103.7 0.6 convolution_bitcast_fusion
  104.2 0.1 slice.63
  104.3 0.0 copy-start.4
  104.3 0.7 multiply_reduce_fusion
  105.0 0.4 copy-done.4
  105.3 0.5 fusion.6
  105.9 0.1 pad_maximum_fusion
  106.0 1.0 copy.34
  107.0 30.8 %all_to_all.10 = bf16[256,8,256]{2,1,0:T(8,128)(2,1)S(1)} all-to-all(bf16[256,8,256]{2,1,0:T(8,128)(2,1)S(1)} %copy.34), channel_id=1, replica_groups=mesh['seq'=8,'tensor'=4] {'seq'}, dimensions={0} | all-to-all | bytes 2097152 | tf_op jit(solution)/shard_map/all_to_all | solution.py:57
  137.8 0.9 fusion.4
  138.7 0.1 fusion.61
  138.7 9.6 %convolution_convert_fusion = bf16[512,4096]{1,0:T(8,128)(2,1)} fusion(bf16[1024,4096]{1,0:T(8,128)(2,1)} %param.15, bf16[256,1024]{0,1:T(8,128)(2,1)S(1)} %bitcast.41, bf16[256,1024]{0,1:T(8,128)(2,1)S(1)} %bitcast.40), kind=kOutput, calls=%fused_computation.1 | convolution fusion | flops 4299161600 | bytes 13631488 | tf_op jit(solution)/shard_map/dot_general | solution.py:63
  148.4 0.0 reduce-scatter.2.cloned.1.call-update
  148.4 45.1 %reduce-scatter.2.cloned.1.call-done = bf16[512,1024]{1,0:T(8,128)(2,1)} async-done(((bf16[512,4096]{1,0:T(8,128)(2,1)}), bf16[512,1024]{1,0:T(8,128)(2,1)}) %reduce-scatter.2.cloned.1.call-update) | async-done | bytes 1048592 | tf_op jit(solution)/shard_map/reduce_scatter | solution.py:64
  193.5 2.2 %fusion.60 = (bf16[256,1024]{1,0:T(8,128)(2,1)}, bf16[256,1024]{1,0:T(8,128)(2,1)}) fusion(bf16[512,1024]{1,0:T(8,128)(2,1)} %reduce-scatter.2.cloned.1.call-done), kind=kLoop, calls=%fused_computation.75 | loop fusion | bytes 2097152 | tf_op jit(solution)/shard_map/slice | solution.py:67
  (3 shorter events, 0.0 us)
Async XLA Ops:
  7.2 3.0 %copy-start = (bf16[256,1024]{1,0:T(8,128)(2,1)S(1)}, bf16[256,1024]{1,0:T(8,128)(2,1)}, u32[]{:S(2)}) copy-start(bf16[256,1024]{1,0:T(8,128)(2,1)} %param.8) | copy-start | bytes 1572868
  7.2 3.2 %copy-start.1 = (bf16[256,1024]{1,0:T(8,128)(2,1)S(1)}, bf16[256,1024]{1,0:T(8,128)(2,1)}, u32[]{:S(2)}) copy-start(bf16[256,1024]{1,0:T(8,128)(2,1)} %param.9) | copy-start | bytes 1572868
  8.0 2.6 %copy-start.2 = (bf16[256,1024]{1,0:T(8,128)(2,1)S(1)}, bf16[256,1024]{1,0:T(8,128)(2,1)}, u32[]{:S(2)}) copy-start(bf16[256,1024]{1,0:T(8,128)(2,1)} %param.12) | copy-start | bytes 1572868
  10.2 1.0 copy-start.3
  23.9 73.6 %all-to-all-start = ((bf16[256,8,768]{2,1,0:T(8,128)(2,1)}), bf16[256,8,768]{2,1,0:T(8,128)(2,1)S(1)}, u32[]{:S(2)}, u32[]{:S(2)}) async-start(bf16[256,8,768]{2,1,0:T(8,128)(2,1)} %copy.27), calls=%async_computation | async-start | bytes 6291456 | tf_op jit(solution)/shard_map/all_to_all | solution.py:28
  30.1 163.4 %reduce-scatter.2.cloned.1.call-start = ((), (), s32[]{:S(2)}) async-start(), calls=%async_computation.3 | async-start | bytes 5242880 | tf_op jit(solution)/shard_map/reduce_scatter | solution.py:64
  102.1 1.6 copy-start.5
  104.3 1.0 copy-start.4
Sparse Core Ops, SparseCore 0:
  148.5 44.9 reduce-scatter.1

commit v2 on v1

v2 whole, which is shorter than its diff:
```python
import functools

import jax
import jax.numpy as jnp
from jax import lax
from jax.experimental import pallas as pl
from jax.experimental.pallas import tpu as pltpu
from jax.sharding import PartitionSpec as P

HEAD_SIZE = 128
MESH = pl.DeviceIdType.MESH


def dot(a, b, contract):
    return lax.dot_general(
        a, b, (((contract[0],), (contract[1],)), ((), ())), preferred_element_type=jnp.float32
    )


def attend(rows):
    e = HEAD_SIZE
    scale = e**-0.5
    count = rows.shape[0]
    query, key = rows[:, e : 2 * e], rows[:, 2 * e : 3 * e]
    scores = dot(query, key, (1, 1)) * scale
    tangent = dot(rows[:, : 2 * e], rows[:, 2 * e : 4 * e], (1, 1)) * scale
    visible = lax.broadcasted_iota(jnp.int32, (count, count), 1) <= lax.broadcasted_iota(
        jnp.int32, (count, count), 0
    )
    masked = jnp.where(visible, scores, -jnp.inf)
    expo = jnp.exp(masked - jnp.max(masked, -1, keepdims=True))
    probs = expo / jnp.sum(expo, -1, keepdims=True)
    slope = probs * (tangent - jnp.sum(probs * tangent, -1, keepdims=True))
    both = dot(probs.astype(jnp.bfloat16), rows[:, 4 * e :], (1, 0))
    extra = dot(slope.astype(jnp.bfloat16), rows[:, 4 * e : 5 * e], (1, 0))
    return jnp.concatenate([both[:, :e], both[:, e:] + extra], 1).astype(jnp.bfloat16)


def kernel(
    n,
    parts,
    q_ref,
    k_ref,
    v_ref,
    dq_ref,
    dk_ref,
    dv_ref,
    routes_ref,
    weight_hbm,
    out_ref,
    tan_ref,
    order,
    sent,
    got,
    result,
    back,
    weight,
    acts,
    own,
    pair_send,
    pair_recv,
    far_send,
    far_recv,
    weight_sem,
    go_send,
    go_recv,
    back_send,
    back_recv,
    pair_sems,
    far_sems,
):
    e = HEAD_SIZE
    tok, width = q_ref.shape
    heads = width // e
    per = tok // n
    groups = parts // 2
    me = lax.axis_index("seq")
    mine = lax.axis_index("tensor")
    group, core = lax.div(mine, 2), lax.rem(mine, 2)
    mate = 2 * group + 1 - core

    barrier = pltpu.get_barrier_semaphore()
    for d in range(1, n):
        pl.semaphore_signal(
            barrier, inc=1, device_id={"seq": lax.rem(me + d, n)}, device_id_type=MESH
        )
    pl.semaphore_signal(barrier, inc=1, device_id={"tensor": mate}, device_id_type=MESH)
    for d in range(1, groups):
        pl.semaphore_signal(
            barrier,
            inc=1,
            device_id={"tensor": 2 * lax.rem(group + d, groups) + core},
            device_id_type=MESH,
        )
    load = pltpu.make_async_copy(weight_hbm, weight, weight_sem)
    load.start()

    row_at = lax.broadcasted_iota(jnp.int32, (tok, tok), 0)
    earlier = (row_at < lax.broadcasted_iota(jnp.int32, (tok, tok), 1)).astype(jnp.float32)
    earlier = earlier.astype(jnp.bfloat16)
    cluster = lax.broadcasted_iota(jnp.int32, (n, tok), 0)

    def place(h, _):
        dest = jnp.right_shift(routes_ref[h], tok.bit_length() - 1)
        member = (dest == cluster).astype(jnp.float32)
        rank = dot(member.astype(jnp.bfloat16), earlier, (1, 0))
        at = jnp.sum(member * (rank + (per * cluster).astype(jnp.float32)), 0, keepdims=True)
        order[h] = (row_at.astype(jnp.float32) == at).astype(jnp.float32).astype(jnp.bfloat16)
        return 0

    lax.fori_loop(0, heads, place, 0)
    pl.semaphore_wait(barrier, n - 1 + groups)

    def go(h, d):
        peer = lax.rem(me + d, n)
        return pltpu.make_async_remote_copy(
            src_ref=sent.at[h, peer],
            dst_ref=got.at[h, me],
            send_sem=go_send.at[h, d],
            recv_sem=go_recv.at[h, d],
            device_id={"seq": peer},
            device_id_type=MESH,
        )

    def come(h, d):
        peer = lax.rem(me + d, n)
        return pltpu.make_async_remote_copy(
            src_ref=result.at[h, peer],
            dst_ref=back.at[h, me],
            send_sem=back_send.at[h, d],
            recv_sem=back_recv.at[h, d],
            device_id={"seq": peer},
            device_id_type=MESH,
        )

    def scatter(h, _):
        cols = pl.ds(pl.multiple_of(h * e, e), e)
        rows = jnp.concatenate(
            [r[:, cols] for r in (dq_ref, q_ref, k_ref, dk_ref, v_ref, dv_ref)], 1
        )
        placed = dot(order[h], rows, (1, 0)).astype(jnp.bfloat16)
        sent[h] = placed.reshape(n, per, 6 * e)
        got[h, me] = sent[h, me]

        def start(d, _):
            go(h, d).start()
            return 0

        lax.fori_loop(1, n, start, 0)
        return 0

    lax.fori_loop(0, heads, scatter, 0)

    def work(h, _):
        def wait(d, _):
            go(h, d).wait()
            return 0

        lax.fori_loop(1, n, wait, 0)
        result[h] = attend(got[h].reshape(tok, 6 * e)).reshape(n, per, 2 * e)
        back[h, me] = result[h, me]

        def start(d, _):
            come(h, d).start()
            return 0

        lax.fori_loop(1, n, start, 0)
        return 0

    lax.fori_loop(0, heads, work, 0)

    def home(h, _):
        def wait(d, _):
            come(h, d).wait()
            return 0

        lax.fori_loop(1, n, wait, 0)
        rows = dot(order[h], back[h].reshape(tok, 2 * e), (0, 0)).astype(jnp.bfloat16)
        cols = pl.ds(pl.multiple_of(h * e, e), e)
        acts[:tok, cols] = rows[:, :e]
        acts[tok:, cols] = rows[:, e:]
        return 0

    lax.fori_loop(0, heads, home, 0)
    load.wait()
    project(groups, group, core, mate, weight, acts, own, pair_send, pair_recv, far_send,
            far_recv, pair_sems, far_sems, out_ref, tan_ref)


def project(groups, group, core, mate, weight, acts, own, pair_send, pair_recv, far_send,
            far_recv, pair_sems, far_sems, out_ref, tan_ref):
    tok, width = out_ref.shape
    tile = min(256, width)

    def product(block, store):
        def step(i, _):
            at = pl.multiple_of(i * tile, tile)
            source = pl.ds(pl.multiple_of(block * width + at, tile), tile)
            store(pl.ds(at, tile), dot(acts[...], weight[:, source], (1, 0)))
            return 0

        lax.fori_loop(0, width // tile, step, 0)

    def to_mate(i):
        return pltpu.make_async_remote_copy(
            src_ref=pair_send.at[i],
            dst_ref=pair_recv.at[i],
            send_sem=pair_sems.at[0, i],
            recv_sem=pair_sems.at[1, i],
            device_id={"tensor": mate},
            device_id_type=MESH,
        )

    def to_far(i):
        return pltpu.make_async_remote_copy(
            src_ref=far_send.at[i],
            dst_ref=far_recv.at[i],
            send_sem=far_sems.at[0, i],
            recv_sem=far_sems.at[1, i],
            device_id={"tensor": 2 * lax.rem(group + 1 + i, groups) + core},
            device_id_type=MESH,
        )

    for i in range(groups):
        there = lax.rem(group + 1 + i, groups)

        def keep_pair(cols, value, i=i):
            pair_send[i, :, cols] = value.astype(jnp.bfloat16)

        product(2 * there + 1 - core, keep_pair)
        to_mate(i).start()

        def keep_own(cols, value, i=i):
            own[i, :, cols] = value

        product(2 * there + core, keep_own)
        if i < groups - 1:
            to_mate(i).wait()
            far_send[i] = (own[i] + pair_recv[i].astype(jnp.float32)).astype(jnp.bfloat16)
            to_far(i).start()
    last = groups - 1
    to_mate(last).wait()
    own[last] = own[last] + pair_recv[last].astype(jnp.float32)
    for i in range(groups - 1):
        to_far(i).wait()
        own[last] = own[last] + far_recv[i].astype(jnp.float32)
    out_ref[...] = own[last, :tok].astype(jnp.bfloat16)
    tan_ref[...] = own[last, tok:].astype(jnp.bfloat16)


def body(n, parts, q, k, v, dq, dk, dv, routes, weight):
    tok, heads = routes.shape
    e = HEAD_SIZE
    per = tok // n
    groups = parts // 2
    width = weight.shape[1] // parts
    half = jnp.bfloat16
    vmem = pl.BlockSpec(memory_space=pltpu.VMEM)
    dma = pltpu.SemaphoreType.DMA
    shape = jax.ShapeDtypeStruct((tok, width), half)
    return pl.pallas_call(
        functools.partial(kernel, n, parts),
        out_shape=(shape, shape),
        in_specs=[vmem] * 7 + [pl.BlockSpec(memory_space=pl.ANY)],
        out_specs=(vmem, vmem),
        scratch_shapes=[
            pltpu.VMEM((heads, tok, tok), half),
            pltpu.VMEM((heads, n, per, 6 * e), half),
            pltpu.VMEM((heads, n, per, 6 * e), half),
            pltpu.VMEM((heads, n, per, 2 * e), half),
            pltpu.VMEM((heads, n, per, 2 * e), half),
            pltpu.VMEM(weight.shape, half),
            pltpu.VMEM((2 * tok, heads * e), half),
            pltpu.VMEM((groups, 2 * tok, width), jnp.float32),
            pltpu.VMEM((groups, 2 * tok, width), half),
            pltpu.VMEM((groups, 2 * tok, width), half),
            pltpu.VMEM((max(groups - 1, 1), 2 * tok, width), half),
            pltpu.VMEM((max(groups - 1, 1), 2 * tok, width), half),
            dma,
            dma((heads, n)),
            dma((heads, n)),
            dma((heads, n)),
            dma((heads, n)),
            dma((2, groups)),
            dma((2, max(groups - 1, 1))),
        ],
        compiler_params=pltpu.CompilerParams(
            collective_id=0, has_side_effects=True, vmem_limit_bytes=56 * 2**20
        ),
    )(q, k, v, dq, dk, dv, routes.T.reshape(heads, 1, tok), weight)


def solution(mesh):
    n, parts = mesh.shape["seq"], mesh.shape["tensor"]
    return jax.shard_map(
        lambda *args: body(n, parts, *args),
        mesh=mesh,
        in_specs=(P("seq", "tensor"),) * 7 + (P("tensor", None),),
        out_specs=(P("seq", "tensor"), P("seq", "tensor")),
        check_vma=False,
    )
```

time: 205 us -> 138 us (0.67)
  the two profiles are of different devices: /device:TPU:16 before, /device:TPU:0 now
where the time goes in v2:
time: 138 us
  Pallas kernels  132 us (96%)
  local copies, waits for them, and re-layouts  5.04 us (4%)
    pallas_call x1, Pallas kernels, body(): pl.pallas_call(functools.partial(kernel, n, parts), out_shape=(shape, sha...  132 us
    unnamed x2, local copies, waits for them, and re-layouts  3.74 us

profile of v2, /device:TPU:0, one launch (start us, length us, event | category | flops | bytes accessed | tf_op | source)
XLA Modules:
  0.0 137.9 jit_solution(3927495805486595086)
XLA Ops:
  0.6 1.3 reshape.7.routes_ref
  1.9 132.2 %shard_map.95 = (bf16[256,1024]{1,0:T(8,128)(2,1)}, bf16[256,1024]{1,0:T(8,128)(2,1)}) custom-call(bf16[256,1024]{1,0:T(8,128)(2,1)} %q_ref.1, bf16[256,1024]{1,0:T(8,128)(2,1)} %k_ref.1, bf16[256,1024]{1,0:T(8,128)(2,1)} %v_ref.1, bf16[256,1024]{1,0:T(8,128)(2,1)} %dq_ref.1, bf16[256,1024]{1,0:T(8,128)(2,1)} %dk_ref.1, bf16[256,1024]{1,0:T(8,128)(2,1)} %dv_ref.1, ...), custom_call_target="tpu_custom_call" | custom-call | tf_op jit(solution)/shard_map/pallas_call | solution.py:261
  134.1 1.9 %copy.12 = bf16[256,1024]{1,0:T(8,128)(2,1)} copy(bf16[256,1024]{1,0:T(8,128)(2,1)} %get-tuple-element.4) | data formatting | bytes 1048576
  136.0 1.9 %copy.13 = bf16[256,1024]{1,0:T(8,128)(2,1)} copy(bf16[256,1024]{1,0:T(8,128)(2,1)} %get-tuple-element.5) | data formatting | bytes 1048576

commit v3 on v2

--- a/solution.py
+++ b/solution.py
@@ -290,10 +290,446 @@
     )(q, k, v, dq, dk, dv, routes.T.reshape(heads, 1, tok), weight)
 
 
+LEVELS = 4
+
+
+def soft_rows(query, keys, offset):
+    e = HEAD_SIZE
+    scale = e**-0.5
+    shape = (query.shape[0], keys.shape[0])
+    scores = dot(query[:, e:], keys[:, :e], (1, 1)) * scale
+    tangent = dot(query, keys[:, : 2 * e], (1, 1)) * scale
+    visible = (
+        lax.broadcasted_iota(jnp.int32, shape, 1)
+        <= lax.broadcasted_iota(jnp.int32, shape, 0) + offset
+    )
+    masked = jnp.where(visible, scores, -jnp.inf)
+    top = jnp.max(masked, -1, keepdims=True)
+    expo = jnp.exp(masked - top)
+    total = jnp.sum(expo, -1, keepdims=True)
+    probs = expo / total
+    mean = jnp.sum(probs * tangent, -1, keepdims=True)
+    slope = probs * (tangent - mean)
+    both = dot(probs.astype(jnp.bfloat16), keys[:, 2 * e :], (1, 0))
+    extra = dot(slope.astype(jnp.bfloat16), keys[:, 2 * e : 3 * e], (1, 0))
+    rows = jnp.concatenate([both[:, :e], both[:, e:] + extra], 1)
+    return rows, top + jnp.log(total), mean
+
+
+def pack_stats(level, mean):
+    lane = lax.broadcasted_iota(jnp.int32, (level.shape[0], 128), 1)
+    return jnp.where(lane == 0, level, jnp.where(lane == 1, mean, 0.0))
+
+
+def merge(pieces):
+    e = HEAD_SIZE
+    top = functools.reduce(jnp.maximum, [level for _, level, _ in pieces])
+    weights = [jnp.exp(level - top) for _, level, _ in pieces]
+    total = functools.reduce(jnp.add, weights)
+    weights = [w / total for w in weights]
+    mean = sum(w * m for w, (_, _, m) in zip(weights, pieces))
+    value = sum(w * rows[:, :e] for w, (rows, _, _) in zip(weights, pieces))
+    slope = sum(
+        w * (rows[:, e:] + (m - mean) * rows[:, :e]) for w, (rows, _, m) in zip(weights, pieces)
+    )
+    return jnp.concatenate([value, slope], 1)
+
+
+def level_kernel(
+    parts,
+    q_ref,
+    k_ref,
+    v_ref,
+    dq_ref,
+    dk_ref,
+    dv_ref,
+    routes_ref,
+    weight_hbm,
+    out_ref,
+    tan_ref,
+    order,
+    sent,
+    rows_here,
+    keys_in,
+    query_in,
+    piece_out,
+    piece_in,
+    stats_out,
+    stats_in,
+    own_piece,
+    own_stats,
+    result,
+    back,
+    weight,
+    acts,
+    own,
+    pair_send,
+    pair_recv,
+    far_send,
+    far_recv,
+    weight_sem,
+    side_sems,
+    key_sems,
+    query_sems,
+    piece_sems,
+    stats_sems,
+    back_sems,
+    pair_sems,
+    far_sems,
+):
+    e = HEAD_SIZE
+    tok, width = q_ref.shape
+    heads = width // e
+    n = 2 * LEVELS
+    per = tok // n
+    here = heads // 2
+    steps = 2 * here
+    some = n // 2
+    groups = parts // 2
+    me = lax.axis_index("seq")
+    mine = lax.axis_index("tensor")
+    level, side = lax.div(me, 2), lax.rem(me, 2)
+    group, core = lax.div(mine, 2), lax.rem(mine, 2)
+    mate = 2 * group + 1 - core
+
+    barrier = pltpu.get_barrier_semaphore()
+    for d in range(1, LEVELS):
+        peer = 2 * lax.rem(level + d, LEVELS) + side
+        pl.semaphore_signal(barrier, inc=1, device_id={"seq": peer}, device_id_type=MESH)
+    pl.semaphore_signal(
+        barrier, inc=1, device_id={"seq": 2 * level + 1 - side}, device_id_type=MESH
+    )
+    pl.semaphore_signal(barrier, inc=1, device_id={"tensor": mate}, device_id_type=MESH)
+    for d in range(1, groups):
+        pl.semaphore_signal(
+            barrier,
+            inc=1,
+            device_id={"tensor": 2 * lax.rem(group + d, groups) + core},
+            device_id_type=MESH,
+        )
+    load = pltpu.make_async_copy(weight_hbm, weight, weight_sem)
+    load.start()
+
+    row_at = lax.broadcasted_iota(jnp.int32, (tok, tok), 0)
+    earlier = (row_at < lax.broadcasted_iota(jnp.int32, (tok, tok), 1)).astype(jnp.float32)
+    earlier = earlier.astype(jnp.bfloat16)
+    cluster = lax.broadcasted_iota(jnp.int32, (n, tok), 0)
+
+    def place(h, _):
+        dest = jnp.right_shift(routes_ref[h], tok.bit_length() - 1)
+        member = (dest == cluster).astype(jnp.float32)
+        rank = dot(member.astype(jnp.bfloat16), earlier, (1, 0))
+        at = jnp.sum(member * (rank + (per * cluster).astype(jnp.float32)), 0, keepdims=True)
+        order[h] = (row_at.astype(jnp.float32) == at).astype(jnp.float32).astype(jnp.bfloat16)
+        return 0
+
+    lax.fori_loop(0, heads, place, 0)
+    pl.semaphore_wait(barrier, LEVELS + groups)
+
+    def remote(src, dst, sems, at, device):
+        return pltpu.make_async_remote_copy(
+            src_ref=src,
+            dst_ref=dst,
+            send_sem=sems.at[(0, *at)],
+            recv_sem=sems.at[(1, *at)],
+            device_id=device,
+            device_id_type=MESH,
+        )
+
+    across = {"seq": 2 * level + 1 - side}
+
+    def at_level(z):
+        return {"seq": 2 * z + side}
+
+    def side_copy(c):
+        return remote(sent.at[c], rows_here.at[c, side], side_sems, (c,), across)
+
+    def key_copy(c):
+        keys = rows_here.at[c, :, :, :, pl.ds(2 * e, 4 * e)]
+        return remote(keys, keys_in.at[c], key_sems, (c,), at_level(1))
+
+    def query_copy(slot, c, z):
+        queries = rows_here.at[c, :, :, :, pl.ds(0, 2 * e)]
+        return remote(queries, query_in.at[slot, c], query_sems, (slot, c), at_level(z))
+
+    def piece_copies(slot, c, z):
+        return (
+            remote(piece_out.at[slot, c], piece_in.at[slot, c], piece_sems, (slot, c), at_level(z)),
+            remote(stats_out.at[slot, c], stats_in.at[slot, c], stats_sems, (slot, c), at_level(z)),
+        )
+
+    def back_copy(c):
+        return remote(result.at[c, 1 - side], back.at[c], back_sems, (c,), across)
+
+    def placed(h, c):
+        cols = pl.ds(pl.multiple_of(h * e, e), e)
+        rows = jnp.concatenate(
+            [r[:, cols] for r in (dq_ref, q_ref, k_ref, dk_ref, v_ref, dv_ref)], 1
+        )
+        half = pl.ds(pl.multiple_of(lax.rem(c, 2) * (tok // 2), tok // 2), tok // 2)
+        moved = dot(order[h, half, :], rows, (1, 0)).astype(jnp.bfloat16)
+        return moved.reshape(some, per, 6 * e)
+
+    def scatter(c, _):
+        sent[c] = placed((1 - side) * here + lax.div(c, 2), c)
+        side_copy(c).start()
+        return 0
+
+    lax.fori_loop(0, steps, scatter, 0)
+
+    def pair_of(ref, i):
+        return jnp.concatenate([ref[0, i], ref[1, i]], 0)
+
+    def finish(c, i, rows):
+        rows = rows.astype(jnp.bfloat16)
+        result[c, 0, i] = rows[:per]
+        result[c, 1, i] = rows[per:]
+
+    def hand_on(slot, c, z, parts_of):
+        for i, (rows, _, _) in enumerate(parts_of):
+            piece_out[slot, c, i] = rows.astype(jnp.bfloat16)
+        packed = pack_stats(
+            jnp.concatenate([p[1] for p in parts_of], 0),
+            jnp.concatenate([p[2] for p in parts_of], 0),
+        )
+        stats_out[slot, c] = packed.T[:8]
+        for copy in piece_copies(slot, c, z):
+            copy.start()
+
+    def keep(c, parts_of):
+        own_piece[c] = jnp.concatenate([p[0] for p in parts_of], 0)
+        own_stats[c] = pack_stats(
+            jnp.concatenate([p[1] for p in parts_of], 0),
+            jnp.concatenate([p[2] for p in parts_of], 0),
+        )
+
+    def advance(c):
+        rows_here[c, side] = placed(side * here + lax.div(c, 2), c)
+        side_copy(c).wait_recv()
+
+        @pl.when(level == 0)
+        def _():
+            key_copy(c).start()
+
+        @pl.when(level == 2)
+        def _():
+            query_copy(0, c, 1).start()
+
+        @pl.when(level == 3)
+        def _():
+            query_copy(0, c, 2).start()
+            query_copy(1, c, 1).start()
+
+    def work(c):
+        own_rows = rows_here.at[c]
+        size = 2 * per
+
+        def cut(piece, j):
+            return tuple(x[j * size : (j + 1) * size] for x in piece)
+
+        @pl.when(level == 0)
+        def _():
+            for i in range(some):
+                rows = pair_of(own_rows, i)
+                finish(c, i, soft_rows(rows[:, : 2 * e], rows[:, 2 * e :], 0)[0])
+            back_copy(c).start()
+
+        @pl.when(level == 1)
+        def _():
+            key_copy(c).wait_recv()
+            query_copy(0, c, 1).wait_recv()
+            query_copy(1, c, 1).wait_recv()
+            pieces = []
+            for i in range(some):
+                rows = pair_of(own_rows, i)
+                queries = jnp.concatenate(
+                    [
+                        rows[:, : 2 * e],
+                        pair_of(query_in.at[0, c], i),
+                        pair_of(query_in.at[1, c], i),
+                    ],
+                    0,
+                )
+                keys = jnp.concatenate([pair_of(keys_in.at[c], i), rows[:, 2 * e :]], 0)
+                pieces.append(soft_rows(queries, keys, size))
+            hand_on(1, c, 3, [cut(p, 2) for p in pieces])
+            hand_on(0, c, 2, [cut(p, 1) for p in pieces])
+            for i in range(some):
+                finish(c, i, pieces[i][0][:size])
+            back_copy(c).start()
+
+        @pl.when(level == 2)
+        def _():
+            query_copy(0, c, 1).wait_recv()
+            pieces = []
+            for i in range(some):
+                rows = pair_of(own_rows, i)
+                queries = jnp.concatenate([rows[:, : 2 * e], pair_of(query_in.at[0, c], i)], 0)
+                pieces.append(soft_rows(queries, rows[:, 2 * e :], 0))
+            hand_on(0, c, 3, [cut(p, 1) for p in pieces])
+            keep(c, [cut(p, 0) for p in pieces])
+
+        @pl.when(level == 3)
+        def _():
+            pieces = []
+            for i in range(some):
+                rows = pair_of(own_rows, i)
+                pieces.append(soft_rows(rows[:, : 2 * e], rows[:, 2 * e :], 0))
+            keep(c, pieces)
+
+    ahead = min(2, steps)
+    for c in range(ahead):
+        advance(c)
+
+    def turn(c, _):
+        @pl.when(c + ahead < steps)
+        def _():
+            advance(c + ahead)
+
+        work(c)
+        return 0
+
+    lax.fori_loop(0, steps, turn, 0)
+
+    def gather(c, slots):
+        pieces = [(own_piece[c], own_stats[c, :, 0:1], own_stats[c, :, 1:2])]
+        for slot in slots:
+            for copy in piece_copies(slot, c, 2):
+                copy.wait_recv()
+            stats = stats_in[slot, c]
+            stats = jnp.concatenate([stats, jnp.zeros((120, stats.shape[1]), jnp.float32)], 0).T
+            rows = piece_in[slot, c].reshape(some * 2 * per, 2 * e).astype(jnp.float32)
+            pieces.append((rows, stats[:, 0:1], stats[:, 1:2]))
+        rows = merge(pieces)
+        for i in range(some):
+            finish(c, i, rows[i * 2 * per : (i + 1) * 2 * per])
+        back_copy(c).start()
+
+    @pl.when(level == 2)
+    def _():
+        lax.fori_loop(0, steps, lambda c, _: (gather(c, (0,)), 0)[1], 0)
+
+    @pl.when(level == 3)
+    def _():
+        lax.fori_loop(0, steps, lambda c, _: (gather(c, (0, 1)), 0)[1], 0)
+
+    def to_acts(h, rows):
+        rows = dot(order[h], rows, (0, 0)).astype(jnp.bfloat16)
+        cols = pl.ds(pl.multiple_of(h * e, e), e)
+        acts[:tok, cols] = rows[:, :e]
+        acts[tok:, cols] = rows[:, e:]
+
+    def both_halves(first, second):
+        return jnp.concatenate([first.reshape(tok // 2, 2 * e), second.reshape(tok // 2, 2 * e)], 0)
+
+    def home(j, _):
+        to_acts(side * here + j, both_halves(result[2 * j, side], result[2 * j + 1, side]))
+        back_copy(2 * j).wait_recv()
+        back_copy(2 * j + 1).wait_recv()
+        to_acts((1 - side) * here + j, both_halves(back[2 * j], back[2 * j + 1]))
+        return 0
+
+    lax.fori_loop(0, here, home, 0)
+    load.wait()
+    project(groups, group, core, mate, weight, acts, own, pair_send, pair_recv, far_send,
+            far_recv, pair_sems, far_sems, out_ref, tan_ref)
+
+    def drain(c, _):
+        side_copy(c).wait_send()
+        back_copy(c).wait_send()
+
+        @pl.when(level == 0)
+        def _():
+            key_copy(c).wait_send()
+
+        @pl.when(level == 1)
+        def _():
+            for slot in (0, 1):
+                for copy in piece_copies(slot, c, 2 + slot):
+                    copy.wait_send()
+
+        @pl.when(level == 2)
+        def _():
+            query_copy(0, c, 1).wait_send()
+            for copy in piece_copies(0, c, 3):
+                copy.wait_send()
+
+        @pl.when(level == 3)
+        def _():
+            query_copy(0, c, 2).wait_send()
+            query_copy(1, c, 1).wait_send()
+
+        return 0
+
+    lax.fori_loop(0, steps, drain, 0)
+
+
+def level_body(parts, q, k, v, dq, dk, dv, routes, weight):
+    tok, heads = routes.shape
+    e = HEAD_SIZE
+    n = 2 * LEVELS
+    per = tok // n
+    steps = heads
+    some = n // 2
+    rows = some * 2 * per
+    groups = parts // 2
+    width = weight.shape[1] // parts
+    half = jnp.bfloat16
+    vmem = pl.BlockSpec(memory_space=pltpu.VMEM)
+    dma = pltpu.SemaphoreType.DMA
+    shape = jax.ShapeDtypeStruct((tok, width), half)
+    return pl.pallas_call(
+        functools.partial(level_kernel, parts),
+        out_shape=(shape, shape),
+        in_specs=[vmem] * 7 + [pl.BlockSpec(memory_space=pl.ANY)],
+        out_specs=(vmem, vmem),
+        scratch_shapes=[
+            pltpu.VMEM((heads, tok, tok), half),
+            pltpu.VMEM((steps, some, per, 6 * e), half),
+            pltpu.VMEM((steps, 2, some, per, 6 * e), half),
+            pltpu.VMEM((steps, 2, some, per, 4 * e), half),
+            pltpu.VMEM((2, steps, 2, some, per, 2 * e), half),
+            pltpu.VMEM((2, steps, some, 2 * per, 2 * e), half),
+            pltpu.VMEM((2, steps, some, 2 * per, 2 * e), half),
+            pltpu.VMEM((2, steps, 8, rows), jnp.float32),
+            pltpu.VMEM((2, steps, 8, rows), jnp.float32),
+            pltpu.VMEM((steps, rows, 2 * e), jnp.float32),
+            pltpu.VMEM((steps, rows, 128), jnp.float32),
+            pltpu.VMEM((steps, 2, some, per, 2 * e), half),
+            pltpu.VMEM((steps, some, per, 2 * e), half),
+            pltpu.VMEM(weight.shape, half),
+            pltpu.VMEM((2 * tok, heads * e), half),
+            pltpu.VMEM((groups, 2 * tok, width), jnp.float32),
+            pltpu.VMEM((groups, 2 * tok, width), half),
+            pltpu.VMEM((groups, 2 * tok, width), half),
+            pltpu.VMEM((max(groups - 1, 1), 2 * tok, width), half),
+            pltpu.VMEM((max(groups - 1, 1), 2 * tok, width), half),
+            dma,
+            dma((2, steps)),
+            dma((2, steps)),
+            dma((2, 2, steps)),
+            dma((2, 2, steps)),
+            dma((2, 2, steps)),
+            dma((2, steps)),
+            dma((2, groups)),
+            dma((2, max(groups - 1, 1))),
+        ],
+        compiler_params=pltpu.CompilerParams(
+            collective_id=1, has_side_effects=True, vmem_limit_bytes=58 * 2**20
+        ),
+    )(q, k, v, dq, dk, dv, routes.T.reshape(heads, 1, tok), weight)
+
+
 def solution(mesh):
     n, parts = mesh.shape["seq"], mesh.shape["tensor"]
+
+    def run(*args):
+        if n == 2 * LEVELS and args[6].shape[1] % 2 == 0:
+            return level_body(parts, *args)
+        return body(n, parts, *args)
+
     return jax.shard_map(
-        lambda *args: body(n, parts, *args),
+        run,
         mesh=mesh,
         in_specs=(P("seq", "tensor"),) * 7 + (P("tensor", None),),
         out_specs=(P("seq", "tensor"), P("seq", "tensor")),

time: 138 us -> 111 us (0.80)
  the two profiles are of different devices: /device:TPU:0 before, /device:TPU:16 now
where the time goes in v3:
time: 111 us
  Pallas kernels  105 us (95%)
  local copies, waits for them, and re-layouts  5.04 us (5%)
    pallas_call x1, Pallas kernels, level_body(): pl.pallas_call(functools.partial(level_kernel, parts), out_shape=(shape,...  105 us
    unnamed x2, local copies, waits for them, and re-layouts  3.74 us

profile of v3, /device:TPU:16, one launch (start us, length us, event | category | flops | bytes accessed | tf_op | source)
XLA Modules:
  0.0 110.7 jit_solution(13319863469671000819)
XLA Ops:
  0.6 1.3 %reshape.7.routes_ref = s32[8,1,256]{2,1,0:T(1,128)} reshape(s32[8,256]{1,0:T(8,128)} %bitcast.1) | data formatting | bytes 16384 | tf_op jit(solution)/shard_map/reshape | solution.py:720
  1.9 105.0 %shard_map.95 = (bf16[256,1024]{1,0:T(8,128)(2,1)}, bf16[256,1024]{1,0:T(8,128)(2,1)}) custom-call(bf16[256,1024]{1,0:T(8,128)(2,1)} %q_ref.1, bf16[256,1024]{1,0:T(8,128)(2,1)} %k_ref.1, bf16[256,1024]{1,0:T(8,128)(2,1)} %v_ref.1, bf16[256,1024]{1,0:T(8,128)(2,1)} %dq_ref.1, bf16[256,1024]{1,0:T(8,128)(2,1)} %dk_ref.1, bf16[256,1024]{1,0:T(8,128)(2,1)} %dv_ref.1, ...), custom_call_target="tpu_custom_call" | custom-call | tf_op jit(solution)/shard_map/pallas_call | solution.py:681
  106.9 1.9 %copy.12 = bf16[256,1024]{1,0:T(8,128)(2,1)} copy(bf16[256,1024]{1,0:T(8,128)(2,1)} %get-tuple-element.4) | data formatting | bytes 1048576
  108.8 1.9 %copy.13 = bf16[256,1024]{1,0:T(8,128)(2,1)} copy(bf16[256,1024]{1,0:T(8,128)(2,1)} %get-tuple-element.5) | data formatting | bytes 1048576

commit v4 on v3

--- a/solution.py
+++ b/solution.py
@@ -9,6 +9,7 @@
 
 HEAD_SIZE = 128
 MESH = pl.DeviceIdType.MESH
+HALVES = 2
 
 
 def dot(a, b, contract):
@@ -48,7 +49,7 @@
     routes_ref,
     weight_hbm,
     out_ref,
-    tan_ref,
+    dest,
     order,
     sent,
     got,
@@ -99,10 +100,12 @@
     earlier = (row_at < lax.broadcasted_iota(jnp.int32, (tok, tok), 1)).astype(jnp.float32)
     earlier = earlier.astype(jnp.bfloat16)
     cluster = lax.broadcasted_iota(jnp.int32, (n, tok), 0)
+    owner = jnp.right_shift(routes_ref[...], tok.bit_length() - 1).astype(jnp.float32)
+    same = (row_at == lax.broadcasted_iota(jnp.int32, (tok, tok), 1)).astype(jnp.float32)
+    dest[...] = dot(owner.astype(jnp.bfloat16), same.astype(jnp.bfloat16), (0, 0))
 
     def place(h, _):
-        dest = jnp.right_shift(routes_ref[h], tok.bit_length() - 1)
-        member = (dest == cluster).astype(jnp.float32)
+        member = (dest[pl.ds(h, 1), :] == cluster.astype(jnp.float32)).astype(jnp.float32)
         rank = dot(member.astype(jnp.bfloat16), earlier, (1, 0))
         at = jnp.sum(member * (rank + (per * cluster).astype(jnp.float32)), 0, keepdims=True)
         order[h] = (row_at.astype(jnp.float32) == at).astype(jnp.float32).astype(jnp.bfloat16)
@@ -184,68 +187,88 @@
     lax.fori_loop(0, heads, home, 0)
     load.wait()
     project(groups, group, core, mate, weight, acts, own, pair_send, pair_recv, far_send,
-            far_recv, pair_sems, far_sems, out_ref, tan_ref)
+            far_recv, pair_sems, far_sems, out_ref)
 
 
 def project(groups, group, core, mate, weight, acts, own, pair_send, pair_recv, far_send,
-            far_recv, pair_sems, far_sems, out_ref, tan_ref):
-    tok, width = out_ref.shape
-    tile = min(256, width)
-
-    def product(block, store):
+            far_recv, pair_sems, far_sems, out_ref):
+    wide = out_ref.shape[1] // HALVES
+    tile = min(256, wide)
+
+    def product(block, half, store):
         def step(i, _):
             at = pl.multiple_of(i * tile, tile)
-            source = pl.ds(pl.multiple_of(block * width + at, tile), tile)
+            first = (block * HALVES + half) * wide
+            source = pl.ds(pl.multiple_of(first + at, tile), tile)
             store(pl.ds(at, tile), dot(acts[...], weight[:, source], (1, 0)))
             return 0
 
-        lax.fori_loop(0, width // tile, step, 0)
-
-    def to_mate(i):
+        lax.fori_loop(0, wide // tile, step, 0)
+
+    def to_mate(i, k):
         return pltpu.make_async_remote_copy(
-            src_ref=pair_send.at[i],
-            dst_ref=pair_recv.at[i],
-            send_sem=pair_sems.at[0, i],
-            recv_sem=pair_sems.at[1, i],
+            src_ref=pair_send.at[i, k],
+            dst_ref=pair_recv.at[i, k],
+            send_sem=pair_sems.at[0, i, k],
+            recv_sem=pair_sems.at[1, i, k],
             device_id={"tensor": mate},
             device_id_type=MESH,
         )
 
-    def to_far(i):
+    def to_far(i, k):
         return pltpu.make_async_remote_copy(
-            src_ref=far_send.at[i],
-            dst_ref=far_recv.at[i],
-            send_sem=far_sems.at[0, i],
-            recv_sem=far_sems.at[1, i],
+            src_ref=far_send.at[i, k],
+            dst_ref=far_recv.at[i, k],
+            send_sem=far_sems.at[0, i, k],
+            recv_sem=far_sems.at[1, i, k],
             device_id={"tensor": 2 * lax.rem(group + 1 + i, groups) + core},
             device_id_type=MESH,
         )
 
+    last = groups - 1
     for i in range(groups):
         there = lax.rem(group + 1 + i, groups)
-
-        def keep_pair(cols, value, i=i):
-            pair_send[i, :, cols] = value.astype(jnp.bfloat16)
-
-        product(2 * there + 1 - core, keep_pair)
-        to_mate(i).start()
-
-        def keep_own(cols, value, i=i):
-            own[i, :, cols] = value
-
-        product(2 * there + core, keep_own)
-        if i < groups - 1:
-            to_mate(i).wait()
-            far_send[i] = (own[i] + pair_recv[i].astype(jnp.float32)).astype(jnp.bfloat16)
-            to_far(i).start()
-    last = groups - 1
-    to_mate(last).wait()
-    own[last] = own[last] + pair_recv[last].astype(jnp.float32)
-    for i in range(groups - 1):
-        to_far(i).wait()
-        own[last] = own[last] + far_recv[i].astype(jnp.float32)
-    out_ref[...] = own[last, :tok].astype(jnp.bfloat16)
-    tan_ref[...] = own[last, tok:].astype(jnp.bfloat16)
+        for k in range(HALVES):
+
+            def keep_pair(cols, value, i=i, k=k):
+                pair_send[i, k, :, cols] = value.astype(jnp.bfloat16)
+
+            product(2 * there + 1 - core, k, keep_pair)
+            to_mate(i, k).start()
+        for k in range(HALVES):
+
+            def keep_own(cols, value, i=i, k=k):
+                own[i, k, :, cols] = value
+
+            product(2 * there + core, k, keep_own)
+            if i < last:
+                to_mate(i, k).wait()
+                total = own[i, k] + pair_recv[i, k].astype(jnp.float32)
+                far_send[i, k] = total.astype(jnp.bfloat16)
+                to_far(i, k).start()
+    for k in range(HALVES):
+        to_mate(last, k).wait()
+        own[last, k] = own[last, k] + pair_recv[last, k].astype(jnp.float32)
+    for k in range(HALVES):
+        total = own[last, k]
+        for i in range(last):
+            to_far(i, k).wait()
+            total = total + far_recv[i, k].astype(jnp.float32)
+        out_ref[:, k * wide : (k + 1) * wide] = total.astype(jnp.bfloat16)
+
+
+def split_kernel(both_ref, out_ref, tan_ref):
+    tok = out_ref.shape[0]
+    out_ref[...] = both_ref[:tok]
+    tan_ref[...] = both_ref[tok:]
+
+
+def split(both):
+    vmem = pl.BlockSpec(memory_space=pltpu.VMEM)
+    shape = jax.ShapeDtypeStruct((both.shape[0] // 2, both.shape[1]), both.dtype)
+    return pl.pallas_call(
+        split_kernel, out_shape=(shape, shape), in_specs=[vmem], out_specs=(vmem, vmem)
+    )(both)
 
 
 def body(n, parts, q, k, v, dq, dk, dv, routes, weight):
@@ -257,13 +280,14 @@
     half = jnp.bfloat16
     vmem = pl.BlockSpec(memory_space=pltpu.VMEM)
     dma = pltpu.SemaphoreType.DMA
-    shape = jax.ShapeDtypeStruct((tok, width), half)
-    return pl.pallas_call(
+    shape = jax.ShapeDtypeStruct((2 * tok, width), half)
+    both = pl.pallas_call(
         functools.partial(kernel, n, parts),
-        out_shape=(shape, shape),
+        out_shape=shape,
         in_specs=[vmem] * 7 + [pl.BlockSpec(memory_space=pl.ANY)],
-        out_specs=(vmem, vmem),
+        out_specs=vmem,
         scratch_shapes=[
+            pltpu.VMEM((heads, tok), jnp.float32),
             pltpu.VMEM((heads, tok, tok), half),
             pltpu.VMEM((heads, n, per, 6 * e), half),
             pltpu.VMEM((heads, n, per, 6 * e), half),
@@ -271,26 +295,28 @@
             pltpu.VMEM((heads, n, per, 2 * e), half),
             pltpu.VMEM(weight.shape, half),
             pltpu.VMEM((2 * tok, heads * e), half),
-            pltpu.VMEM((groups, 2 * tok, width), jnp.float32),
-            pltpu.VMEM((groups, 2 * tok, width), half),
-            pltpu.VMEM((groups, 2 * tok, width), half),
-            pltpu.VMEM((max(groups - 1, 1), 2 * tok, width), half),
-            pltpu.VMEM((max(groups - 1, 1), 2 * tok, width), half),
+            pltpu.VMEM((groups, HALVES, 2 * tok, width // HALVES), jnp.float32),
+            pltpu.VMEM((groups, HALVES, 2 * tok, width // HALVES), half),
+            pltpu.VMEM((groups, HALVES, 2 * tok, width // HALVES), half),
+            pltpu.VMEM((max(groups - 1, 1), HALVES, 2 * tok, width // HALVES), half),
+            pltpu.VMEM((max(groups - 1, 1), HALVES, 2 * tok, width // HALVES), half),
             dma,
             dma((heads, n)),
             dma((heads, n)),
             dma((heads, n)),
             dma((heads, n)),
-            dma((2, groups)),
-            dma((2, max(groups - 1, 1))),
+            dma((2, groups, HALVES)),
+            dma((2, max(groups - 1, 1), HALVES)),
         ],
         compiler_params=pltpu.CompilerParams(
             collective_id=0, has_side_effects=True, vmem_limit_bytes=56 * 2**20
         ),
-    )(q, k, v, dq, dk, dv, routes.T.reshape(heads, 1, tok), weight)
+    )(q, k, v, dq, dk, dv, routes, weight)
+    return split(both)
 
 
 LEVELS = 4
+CUTS = 4
 
 
 def soft_rows(query, keys, offset):
@@ -346,7 +372,7 @@
     routes_ref,
     weight_hbm,
     out_ref,
-    tan_ref,
+    dest,
     order,
     sent,
     rows_here,
@@ -383,8 +409,8 @@
     n = 2 * LEVELS
     per = tok // n
     here = heads // 2
-    steps = 2 * here
-    some = n // 2
+    steps = CUTS * here
+    some = n // CUTS
     groups = parts // 2
     me = lax.axis_index("seq")
     mine = lax.axis_index("tensor")
@@ -414,10 +440,12 @@
     earlier = (row_at < lax.broadcasted_iota(jnp.int32, (tok, tok), 1)).astype(jnp.float32)
     earlier = earlier.astype(jnp.bfloat16)
     cluster = lax.broadcasted_iota(jnp.int32, (n, tok), 0)
+    owner = jnp.right_shift(routes_ref[...], tok.bit_length() - 1).astype(jnp.float32)
+    same = (row_at == lax.broadcasted_iota(jnp.int32, (tok, tok), 1)).astype(jnp.float32)
+    dest[...] = dot(owner.astype(jnp.bfloat16), same.astype(jnp.bfloat16), (0, 0))
 
     def place(h, _):
-        dest = jnp.right_shift(routes_ref[h], tok.bit_length() - 1)
-        member = (dest == cluster).astype(jnp.float32)
+        member = (dest[pl.ds(h, 1), :] == cluster.astype(jnp.float32)).astype(jnp.float32)
         rank = dot(member.astype(jnp.bfloat16), earlier, (1, 0))
         at = jnp.sum(member * (rank + (per * cluster).astype(jnp.float32)), 0, keepdims=True)
         order[h] = (row_at.astype(jnp.float32) == at).astype(jnp.float32).astype(jnp.bfloat16)
@@ -466,12 +494,13 @@
         rows = jnp.concatenate(
             [r[:, cols] for r in (dq_ref, q_ref, k_ref, dk_ref, v_ref, dv_ref)], 1
         )
-        half = pl.ds(pl.multiple_of(lax.rem(c, 2) * (tok // 2), tok // 2), tok // 2)
-        moved = dot(order[h, half, :], rows, (1, 0)).astype(jnp.bfloat16)
+        size = tok // CUTS
+        cut = pl.ds(pl.multiple_of(lax.rem(c, CUTS) * size, size), size)
+        moved = dot(order[h, cut, :], rows, (1, 0)).astype(jnp.bfloat16)
         return moved.reshape(some, per, 6 * e)
 
     def scatter(c, _):
-        sent[c] = placed((1 - side) * here + lax.div(c, 2), c)
+        sent[c] = placed((1 - side) * here + lax.div(c, CUTS), c)
         side_copy(c).start()
         return 0
 
@@ -504,7 +533,7 @@
         )
 
     def advance(c):
-        rows_here[c, side] = placed(side * here + lax.div(c, 2), c)
+        rows_here[c, side] = placed(side * here + lax.div(c, CUTS), c)
         side_copy(c).wait_recv()
 
         @pl.when(level == 0)
@@ -619,20 +648,22 @@
         acts[:tok, cols] = rows[:, :e]
         acts[tok:, cols] = rows[:, e:]
 
-    def both_halves(first, second):
-        return jnp.concatenate([first.reshape(tok // 2, 2 * e), second.reshape(tok // 2, 2 * e)], 0)
-
     def home(j, _):
-        to_acts(side * here + j, both_halves(result[2 * j, side], result[2 * j + 1, side]))
-        back_copy(2 * j).wait_recv()
-        back_copy(2 * j + 1).wait_recv()
-        to_acts((1 - side) * here + j, both_halves(back[2 * j], back[2 * j + 1]))
+        def whole(at):
+            return jnp.concatenate(
+                [at(CUTS * j + p).reshape(tok // CUTS, 2 * e) for p in range(CUTS)], 0
+            )
+
+        to_acts(side * here + j, whole(lambda c: result[c, side]))
+        for p in range(CUTS):
+            back_copy(CUTS * j + p).wait_recv()
+        to_acts((1 - side) * here + j, whole(lambda c: back[c]))
         return 0
 
     lax.fori_loop(0, here, home, 0)
     load.wait()
     project(groups, group, core, mate, weight, acts, own, pair_send, pair_recv, far_send,
-            far_recv, pair_sems, far_sems, out_ref, tan_ref)
+            far_recv, pair_sems, far_sems, out_ref)
 
     def drain(c, _):
         side_copy(c).wait_send()
@@ -669,21 +700,22 @@
     e = HEAD_SIZE
     n = 2 * LEVELS
     per = tok // n
-    steps = heads
-    some = n // 2
+    steps = CUTS * (heads // 2)
+    some = n // CUTS
     rows = some * 2 * per
     groups = parts // 2
     width = weight.shape[1] // parts
     half = jnp.bfloat16
     vmem = pl.BlockSpec(memory_space=pltpu.VMEM)
     dma = pltpu.SemaphoreType.DMA
-    shape = jax.ShapeDtypeStruct((tok, width), half)
-    return pl.pallas_call(
+    shape = jax.ShapeDtypeStruct((2 * tok, width), half)
+    both = pl.pallas_call(
         functools.partial(level_kernel, parts),
-        out_shape=(shape, shape),
+        out_shape=shape,
         in_specs=[vmem] * 7 + [pl.BlockSpec(memory_space=pl.ANY)],
-        out_specs=(vmem, vmem),
+        out_specs=vmem,
         scratch_shapes=[
+            pltpu.VMEM((heads, tok), jnp.float32),
             pltpu.VMEM((heads, tok, tok), half),
             pltpu.VMEM((steps, some, per, 6 * e), half),
             pltpu.VMEM((steps, 2, some, per, 6 * e), half),
@@ -699,11 +731,11 @@
             pltpu.VMEM((steps, some, per, 2 * e), half),
             pltpu.VMEM(weight.shape, half),
             pltpu.VMEM((2 * tok, heads * e), half),
-            pltpu.VMEM((groups, 2 * tok, width), jnp.float32),
-            pltpu.VMEM((groups, 2 * tok, width), half),
-            pltpu.VMEM((groups, 2 * tok, width), half),
-            pltpu.VMEM((max(groups - 1, 1), 2 * tok, width), half),
-            pltpu.VMEM((max(groups - 1, 1), 2 * tok, width), half),
+            pltpu.VMEM((groups, HALVES, 2 * tok, width // HALVES), jnp.float32),
+            pltpu.VMEM((groups, HALVES, 2 * tok, width // HALVES), half),
+            pltpu.VMEM((groups, HALVES, 2 * tok, width // HALVES), half),
+            pltpu.VMEM((max(groups - 1, 1), HALVES, 2 * tok, width // HALVES), half),
+            pltpu.VMEM((max(groups - 1, 1), HALVES, 2 * tok, width // HALVES), half),
             dma,
             dma((2, steps)),
             dma((2, steps)),
@@ -711,13 +743,14 @@
             dma((2, 2, steps)),
             dma((2, 2, steps)),
             dma((2, steps)),
-            dma((2, groups)),
-            dma((2, max(groups - 1, 1))),
+            dma((2, groups, HALVES)),
+            dma((2, max(groups - 1, 1), HALVES)),
         ],
         compiler_params=pltpu.CompilerParams(
             collective_id=1, has_side_effects=True, vmem_limit_bytes=58 * 2**20
         ),
-    )(q, k, v, dq, dk, dv, routes.T.reshape(heads, 1, tok), weight)
+    )(q, k, v, dq, dk, dv, routes, weight)
+    return split(both)
 
 
 def solution(mesh):

time: 111 us -> 104 us (0.937)
  local copies, waits for them, and re-layouts: 5.04 us -> 1.49 us
  Pallas kernels: 105 us -> 102 us
    pallas_call x1 -> x2, Pallas kernels: 105 us -> 102 us  [the longest x1 99.5 us: level_body(): pl.pallas_call(functools.partial(level_kernel, parts), out_shape=shape, i...]
    unnamed x2 -> x1, local copies, waits for them, and re-layouts: 3.74 us -> 1.49 us
    reshape x1 -> x0, local copies, waits for them, and re-layouts: 1.3 us -> none  [level_body(): routes.T.reshape(heads, 1, tok)]
where the time goes in v4:
time: 104 us
  Pallas kernels  102 us (98%)
  local copies, waits for them, and re-layouts  1.49 us (1%)
    pallas_call x1, Pallas kernels, level_body(): pl.pallas_call(functools.partial(level_kernel, parts), out_shape=shape, i...  99.5 us
    pallas_call x1, Pallas kernels, split(): pl.pallas_call(split_kernel, out_shape=(shape, shape), in_specs=[vmem], o...  2.23 us

profile of v4, /device:TPU:16, one launch (start us, length us, event | category | flops | bytes accessed | tf_op | source)
XLA Modules:
  0.0 103.8 jit_solution(6029373962597234136)
XLA Ops:
  0.6 1.5 %copy.10.routes_ref = s32[256,8]{1,0:T(8,128)} copy(s32[256,8]{0,1:T(8,128)} %param.14) | data formatting | bytes 16384 | tf_op args[6]
  2.1 99.5 %shard_map.95.both_ref = bf16[512,1024]{1,0:T(8,128)(2,1)} custom-call(bf16[256,1024]{1,0:T(8,128)(2,1)} %q_ref.1, bf16[256,1024]{1,0:T(8,128)(2,1)} %k_ref.1, bf16[256,1024]{1,0:T(8,128)(2,1)} %v_ref.1, bf16[256,1024]{1,0:T(8,128)(2,1)} %dq_ref.1, bf16[256,1024]{1,0:T(8,128)(2,1)} %dk_ref.1, bf16[256,1024]{1,0:T(8,128)(2,1)} %dv_ref.1, ...), custom_call_target="tpu_custom_call" | custom-call | tf_op jit(solution)/shard_map/pallas_call | solution.py:712
  101.6 2.2 %shard_map.96 = (bf16[256,1024]{1,0:T(8,128)(2,1)}, bf16[256,1024]{1,0:T(8,128)(2,1)}) custom-call(bf16[512,1024]{1,0:T(8,128)(2,1)} %shard_map.95.both_ref), custom_call_target="tpu_custom_call" | custom-call | tf_op jit(solution)/shard_map/pallas_call | solution.py:269

commit v5 on v4

--- a/solution.py
+++ b/solution.py
@@ -100,9 +100,7 @@
     earlier = (row_at < lax.broadcasted_iota(jnp.int32, (tok, tok), 1)).astype(jnp.float32)
     earlier = earlier.astype(jnp.bfloat16)
     cluster = lax.broadcasted_iota(jnp.int32, (n, tok), 0)
-    owner = jnp.right_shift(routes_ref[...], tok.bit_length() - 1).astype(jnp.float32)
-    same = (row_at == lax.broadcasted_iota(jnp.int32, (tok, tok), 1)).astype(jnp.float32)
-    dest[...] = dot(owner.astype(jnp.bfloat16), same.astype(jnp.bfloat16), (0, 0))
+    dest[...] = jnp.right_shift(routes_ref[...], tok.bit_length() - 1).astype(jnp.float32)
 
     def place(h, _):
         member = (dest[pl.ds(h, 1), :] == cluster.astype(jnp.float32)).astype(jnp.float32)
@@ -311,7 +309,7 @@
         compiler_params=pltpu.CompilerParams(
             collective_id=0, has_side_effects=True, vmem_limit_bytes=56 * 2**20
         ),
-    )(q, k, v, dq, dk, dv, routes, weight)
+    )(q, k, v, dq, dk, dv, routes.T, weight)
     return split(both)
 
 
@@ -440,9 +438,7 @@
     earlier = (row_at < lax.broadcasted_iota(jnp.int32, (tok, tok), 1)).astype(jnp.float32)
     earlier = earlier.astype(jnp.bfloat16)
     cluster = lax.broadcasted_iota(jnp.int32, (n, tok), 0)
-    owner = jnp.right_shift(routes_ref[...], tok.bit_length() - 1).astype(jnp.float32)
-    same = (row_at == lax.broadcasted_iota(jnp.int32, (tok, tok), 1)).astype(jnp.float32)
-    dest[...] = dot(owner.astype(jnp.bfloat16), same.astype(jnp.bfloat16), (0, 0))
+    dest[...] = jnp.right_shift(routes_ref[...], tok.bit_length() - 1).astype(jnp.float32)
 
     def place(h, _):
         member = (dest[pl.ds(h, 1), :] == cluster.astype(jnp.float32)).astype(jnp.float32)
@@ -606,19 +602,23 @@
                 pieces.append(soft_rows(rows[:, : 2 * e], rows[:, 2 * e :], 0))
             keep(c, pieces)
 
-    ahead = min(2, steps)
-    for c in range(ahead):
-        advance(c)
-
-    def turn(c, _):
-        @pl.when(c + ahead < steps)
-        def _():
-            advance(c + ahead)
-
-        work(c)
-        return 0
-
-    lax.fori_loop(0, steps, turn, 0)
+    def to_acts(h, rows):
+        rows = dot(order[h], rows, (0, 0)).astype(jnp.bfloat16)
+        cols = pl.ds(pl.multiple_of(h * e, e), e)
+        acts[:tok, cols] = rows[:, :e]
+        acts[tok:, cols] = rows[:, e:]
+
+    def home(j, _):
+        def whole(at):
+            return jnp.concatenate(
+                [at(CUTS * j + p).reshape(tok // CUTS, 2 * e) for p in range(CUTS)], 0
+            )
+
+        to_acts(side * here + j, whole(lambda c: result[c, side]))
+        for p in range(CUTS):
+            back_copy(CUTS * j + p).wait_recv()
+        to_acts((1 - side) * here + j, whole(lambda c: back[c]))
+        return 0
 
     def gather(c, slots):
         pieces = [(own_piece[c], own_stats[c, :, 0:1], own_stats[c, :, 1:2])]
@@ -634,33 +634,41 @@
             finish(c, i, rows[i * 2 * per : (i + 1) * 2 * per])
         back_copy(c).start()
 
-    @pl.when(level == 2)
-    def _():
-        lax.fori_loop(0, steps, lambda c, _: (gather(c, (0,)), 0)[1], 0)
-
-    @pl.when(level == 3)
-    def _():
-        lax.fori_loop(0, steps, lambda c, _: (gather(c, (0, 1)), 0)[1], 0)
-
-    def to_acts(h, rows):
-        rows = dot(order[h], rows, (0, 0)).astype(jnp.bfloat16)
-        cols = pl.ds(pl.multiple_of(h * e, e), e)
-        acts[:tok, cols] = rows[:, :e]
-        acts[tok:, cols] = rows[:, e:]
-
-    def home(j, _):
-        def whole(at):
-            return jnp.concatenate(
-                [at(CUTS * j + p).reshape(tok // CUTS, 2 * e) for p in range(CUTS)], 0
-            )
-
-        to_acts(side * here + j, whole(lambda c: result[c, side]))
-        for p in range(CUTS):
-            back_copy(CUTS * j + p).wait_recv()
-        to_acts((1 - side) * here + j, whole(lambda c: back[c]))
-        return 0
-
-    lax.fori_loop(0, here, home, 0)
+    def collect(c):
+        @pl.when(level == 2)
+        def _():
+            gather(c, (0,))
+
+        @pl.when(level == 3)
+        def _():
+            gather(c, (0, 1))
+
+    ahead, lag = 2, CUTS
+    for c in range(ahead):
+        advance(c)
+
+    def turn(c, _):
+        @pl.when(c + ahead < steps)
+        def _():
+            advance(c + ahead)
+
+        work(c)
+
+        @pl.when(c >= lag)
+        def _():
+            collect(c - lag)
+
+        return 0
+
+    lax.fori_loop(0, steps, turn, 0)
+    lax.fori_loop(0, here - 1, home, 0)
+
+    def rest(c, _):
+        collect(c)
+        return 0
+
+    lax.fori_loop(steps - lag, steps, rest, 0)
+    home(here - 1, 0)
     load.wait()
     project(groups, group, core, mate, weight, acts, own, pair_send, pair_recv, far_send,
             far_recv, pair_sems, far_sems, out_ref)
@@ -749,7 +757,7 @@
         compiler_params=pltpu.CompilerParams(
             collective_id=1, has_side_effects=True, vmem_limit_bytes=58 * 2**20
         ),
-    )(q, k, v, dq, dk, dv, routes, weight)
+    )(q, k, v, dq, dk, dv, routes.T, weight)
     return split(both)
 
 

time: 104 us -> 102 us (0.981)
  local copies, waits for them, and re-layouts: 1.49 us -> 0 us
    unnamed x1 -> x0, local copies, waits for them, and re-layouts: 1.49 us -> none
where the time goes in v5:
time: 102 us
  Pallas kernels  102 us (100%)
    pallas_call x1, Pallas kernels, level_body(): pl.pallas_call(functools.partial(level_kernel, parts), out_shape=shape, i...  99.3 us
    pallas_call x1, Pallas kernels, split(): pl.pallas_call(split_kernel, out_shape=(shape, shape), in_specs=[vmem], o...  2.23 us

profile of v5, /device:TPU:16, one launch (start us, length us, event | category | flops | bytes accessed | tf_op | source)
XLA Modules:
  0.0 102.2 jit_solution(3143643370699971854)
XLA Ops:
  0.6 99.3 %shard_map.95.both_ref = bf16[512,1024]{1,0:T(8,128)(2,1)} custom-call(bf16[256,1024]{1,0:T(8,128)(2,1)} %q_ref.1, bf16[256,1024]{1,0:T(8,128)(2,1)} %k_ref.1, bf16[256,1024]{1,0:T(8,128)(2,1)} %v_ref.1, bf16[256,1024]{1,0:T(8,128)(2,1)} %dq_ref.1, bf16[256,1024]{1,0:T(8,128)(2,1)} %dk_ref.1, bf16[256,1024]{1,0:T(8,128)(2,1)} %dv_ref.1, s32[8,256]{1,0:T(8,128)} %bitcast.1, ...), custom_call_target="tpu_custom_call" | custom-call | tf_op jit(solution)/shard_map/pallas_call | solution.py:720
  100.0 2.2 %shard_map.96 = (bf16[256,1024]{1,0:T(8,128)(2,1)}, bf16[256,1024]{1,0:T(8,128)(2,1)}) custom-call(bf16[512,1024]{1,0:T(8,128)(2,1)} %shard_map.95.both_ref), custom_call_target="tpu_custom_call" | custom-call | tf_op jit(solution)/shard_map/pallas_call | solution.py:267

commit v6 on v5

--- a/solution.py
+++ b/solution.py
@@ -440,14 +440,13 @@
     cluster = lax.broadcasted_iota(jnp.int32, (n, tok), 0)
     dest[...] = jnp.right_shift(routes_ref[...], tok.bit_length() - 1).astype(jnp.float32)
 
-    def place(h, _):
+    def place(h):
         member = (dest[pl.ds(h, 1), :] == cluster.astype(jnp.float32)).astype(jnp.float32)
         rank = dot(member.astype(jnp.bfloat16), earlier, (1, 0))
         at = jnp.sum(member * (rank + (per * cluster).astype(jnp.float32)), 0, keepdims=True)
         order[h] = (row_at.astype(jnp.float32) == at).astype(jnp.float32).astype(jnp.bfloat16)
-        return 0
-
-    lax.fori_loop(0, heads, place, 0)
+
+    place((1 - side) * here)
     pl.semaphore_wait(barrier, LEVELS + groups)
 
     def remote(src, dst, sems, at, device):
@@ -500,7 +499,8 @@
         side_copy(c).start()
         return 0
 
-    lax.fori_loop(0, steps, scatter, 0)
+    lax.fori_loop(0, CUTS, scatter, 0)
+    place(side * here)
 
     def pair_of(ref, i):
         return jnp.concatenate([ref[0, i], ref[1, i]], 0)
@@ -646,6 +646,14 @@
     ahead, lag = 2, CUTS
     for c in range(ahead):
         advance(c)
+
+    def feed(j, _):
+        place((1 - side) * here + j)
+        lax.fori_loop(CUTS * j, CUTS * (j + 1), scatter, 0)
+        place(side * here + j)
+        return 0
+
+    lax.fori_loop(1, here, feed, 0)
 
     def turn(c, _):
         @pl.when(c + ahead < steps)

time: 102 us -> 102 us (level)
  no operation moved by 1% of the time
where the time goes in v6:
time: 102 us
  Pallas kernels  102 us (100%)
    pallas_call x1, Pallas kernels, level_body(): pl.pallas_call(functools.partial(level_kernel, parts), out_shape=shape, i...  99.4 us
    pallas_call x1, Pallas kernels, split(): pl.pallas_call(split_kernel, out_shape=(shape, shape), in_specs=[vmem], o...  2.23 us

profile of v6, /device:TPU:16, one launch (start us, length us, event | category | flops | bytes accessed | tf_op | source)
XLA Modules:
  0.0 102.2 jit_solution(15887016958931960399)
XLA Ops:
  0.6 99.4 %shard_map.95.both_ref = bf16[512,1024]{1,0:T(8,128)(2,1)} custom-call(bf16[256,1024]{1,0:T(8,128)(2,1)} %q_ref.1, bf16[256,1024]{1,0:T(8,128)(2,1)} %k_ref.1, bf16[256,1024]{1,0:T(8,128)(2,1)} %v_ref.1, bf16[256,1024]{1,0:T(8,128)(2,1)} %dq_ref.1, bf16[256,1024]{1,0:T(8,128)(2,1)} %dk_ref.1, bf16[256,1024]{1,0:T(8,128)(2,1)} %dv_ref.1, s32[8,256]{1,0:T(8,128)} %bitcast.1, ...), custom_call_target="tpu_custom_call" | custom-call | tf_op jit(solution)/shard_map/pallas_call | solution.py:728
  100.0 2.2 %shard_map.96 = (bf16[256,1024]{1,0:T(8,128)(2,1)}, bf16[256,1024]{1,0:T(8,128)(2,1)}) custom-call(bf16[512,1024]{1,0:T(8,128)(2,1)} %shard_map.95.both_ref), custom_call_target="tpu_custom_call" | custom-call | tf_op jit(solution)/shard_map/pallas_call | solution.py:267

commit v7 on v6

--- a/solution.py
+++ b/solution.py
@@ -384,14 +384,19 @@
     own_stats,
     result,
     back,
-    weight,
-    acts,
+    weight_early,
+    weight_late,
+    acts_early,
+    acts_late,
     own,
     pair_send,
     pair_recv,
     far_send,
     far_recv,
-    weight_sem,
+    early_sems,
+    late_sems,
+    weight_sems,
+    acts_sems,
     side_sems,
     key_sems,
     query_sems,
@@ -416,6 +421,11 @@
     group, core = lax.div(mine, 2), lax.rem(mine, 2)
     mate = 2 * group + 1 - core
 
+
+    def tensor_peer(slot):
+        which = core if slot % 2 == 0 else 1 - core
+        return 2 * lax.rem(group + slot // 2, groups) + which
+
     barrier = pltpu.get_barrier_semaphore()
     for d in range(1, LEVELS):
         peer = 2 * lax.rem(level + d, LEVELS) + side
@@ -423,16 +433,34 @@
     pl.semaphore_signal(
         barrier, inc=1, device_id={"seq": 2 * level + 1 - side}, device_id_type=MESH
     )
-    pl.semaphore_signal(barrier, inc=1, device_id={"tensor": mate}, device_id_type=MESH)
-    for d in range(1, groups):
+    for slot in range(1, parts):
         pl.semaphore_signal(
-            barrier,
-            inc=1,
-            device_id={"tensor": 2 * lax.rem(group + d, groups) + core},
-            device_id_type=MESH,
-        )
-    load = pltpu.make_async_copy(weight_hbm, weight, weight_sem)
-    load.start()
+            barrier, inc=1, device_id={"tensor": tensor_peer(slot)}, device_id_type=MESH
+        )
+    early, last = here - 1, groups - 1
+    sides = (0, 1)
+    loads = [
+        pltpu.make_async_copy(
+            weight_hbm.at[pl.ds((w * here + j) * e, e), :],
+            weight_early.at[pl.ds((2 * j + w) * e, e), :],
+            early_sems.at[2 * j + w],
+        )
+        for j in range(early)
+        for w in sides
+    ]
+
+    def late_weight(w, block):
+        rows = pl.ds((w * here + early) * e, e)
+        return weight_hbm.at[rows, pl.ds(pl.multiple_of(block * width, width), width)]
+
+    late_loads = [
+        pltpu.make_async_copy(
+            late_weight(w, mine), weight_late.at[0, pl.ds(w * e, e), :], late_sems.at[w]
+        )
+        for w in sides
+    ]
+    for load in loads + late_loads:
+        load.start()
 
     row_at = lax.broadcasted_iota(jnp.int32, (tok, tok), 0)
     earlier = (row_at < lax.broadcasted_iota(jnp.int32, (tok, tok), 1)).astype(jnp.float32)
@@ -447,7 +475,7 @@
         order[h] = (row_at.astype(jnp.float32) == at).astype(jnp.float32).astype(jnp.bfloat16)
 
     place((1 - side) * here)
-    pl.semaphore_wait(barrier, LEVELS + groups)
+    pl.semaphore_wait(barrier, LEVELS + parts - 1)
 
     def remote(src, dst, sems, at, device):
         return pltpu.make_async_remote_copy(
@@ -501,6 +529,23 @@
 
     lax.fori_loop(0, CUTS, scatter, 0)
     place(side * here)
+
+    def weight_copy(slot, w):
+        peer = tensor_peer(slot)
+        dst = weight_late.at[slot, pl.ds(w * e, e), :]
+        return remote(late_weight(w, peer), dst, weight_sems, (slot, w), {"tensor": peer})
+
+    def acts_copy(slot):
+        device = {"tensor": tensor_peer(slot)}
+        return remote(acts_late.at[0], acts_late.at[slot], acts_sems, (slot,), device)
+
+    def forward(slot):
+        device = {"tensor": mate}
+        return remote(acts_late.at[slot], acts_late.at[slot + 1], acts_sems, (slot + 1,), device)
+
+    for slot in range(1, parts):
+        for w in sides:
+            weight_copy(slot, w).start()
 
     def pair_of(ref, i):
         return jnp.concatenate([ref[0, i], ref[1, i]], 0)
@@ -602,23 +647,121 @@
                 pieces.append(soft_rows(rows[:, : 2 * e], rows[:, 2 * e :], 0))
             keep(c, pieces)
 
-    def to_acts(h, rows):
-        rows = dot(order[h], rows, (0, 0)).astype(jnp.bfloat16)
-        cols = pl.ds(pl.multiple_of(h * e, e), e)
-        acts[:tok, cols] = rows[:, :e]
-        acts[tok:, cols] = rows[:, e:]
-
-    def home(j, _):
+    def home(j, put):
         def whole(at):
             return jnp.concatenate(
                 [at(CUTS * j + p).reshape(tok // CUTS, 2 * e) for p in range(CUTS)], 0
             )
 
-        to_acts(side * here + j, whole(lambda c: result[c, side]))
+        def back_home(w, rows):
+            rows = dot(order[w * here + j], rows, (0, 0)).astype(jnp.bfloat16)
+            put(w, rows[:, :e], rows[:, e:])
+
+        back_home(side, whole(lambda c: result[c, side]))
         for p in range(CUTS):
             back_copy(CUTS * j + p).wait_recv()
-        to_acts((1 - side) * here + j, whole(lambda c: back[c]))
+        back_home(1 - side, whole(lambda c: back[c]))
+
+    def home_early(j, _):
+        def put(w, value, slope):
+            cols = pl.ds(pl.multiple_of((2 * j + w) * e, e), e)
+            acts_early[:tok, cols] = value
+            acts_early[tok:, cols] = slope
+
+        home(j, put)
         return 0
+
+    def put_late(w, value, slope):
+        cols = pl.ds(pl.multiple_of(w * e, e), e)
+        acts_late[0, :tok, cols] = value
+        acts_late[0, tok:, cols] = slope
+
+    wide = width // HALVES
+    tile = min(256, wide)
+
+    def product(block, half, store):
+        def step(i, _):
+            at = pl.multiple_of(i * tile, tile)
+            first = (block * HALVES + half) * wide
+            source = pl.ds(pl.multiple_of(first + at, tile), tile)
+            store(pl.ds(at, tile), dot(acts_early[...], weight_early[:, source], (1, 0)))
+            return 0
+
+        lax.fori_loop(0, wide // tile, step, 0)
+
+    def to_mate(i, k):
+        device = {"tensor": mate}
+        return remote(pair_send.at[i, k], pair_recv.at[i, k], pair_sems, (i, k), device)
+
+    def to_far(i, k):
+        device = {"tensor": 2 * lax.rem(group + 1 + i, groups) + core}
+        return remote(far_send.at[i, k], far_recv.at[i, k], far_sems, (i, k), device)
+
+    def project_early():
+        lax.fori_loop(0, early, home_early, 0)
+        for load in loads:
+            load.wait()
+        for i in range(groups):
+            there = lax.rem(group + 1 + i, groups)
+            for k in range(HALVES):
+
+                def keep_pair(cols, value, i=i, k=k):
+                    pair_send[i, k, :, cols] = value.astype(jnp.bfloat16)
+
+                product(2 * there + 1 - core, k, keep_pair)
+                to_mate(i, k).start()
+            for k in range(HALVES):
+
+                def keep_own(cols, value, i=i, k=k):
+                    own[i, k, :, cols] = value
+
+                product(2 * there + core, k, keep_own)
+                if i < last:
+                    to_mate(i, k).wait()
+                    total = own[i, k] + pair_recv[i, k].astype(jnp.float32)
+                    far_send[i, k] = total.astype(jnp.bfloat16)
+                    to_far(i, k).start()
+
+    def add_late(slot):
+        for k in range(HALVES):
+
+            def step(i, _, k=k):
+                at = pl.multiple_of(i * tile, tile)
+                cols = pl.ds(at, tile)
+                source = pl.ds(pl.multiple_of(k * wide + at, tile), tile)
+                more = dot(acts_late[slot], weight_late[slot, :, source], (1, 0))
+                own[last, k, :, cols] = own[last, k, :, cols] + more
+                return 0
+
+            lax.fori_loop(0, wide // tile, step, 0)
+
+    def project_late():
+        for slot in [2 * d for d in range(1, groups)] + [1]:
+            acts_copy(slot).start()
+        for k in range(HALVES):
+            to_mate(last, k).wait()
+            own[last, k] = own[last, k] + pair_recv[last, k].astype(jnp.float32)
+        for load in late_loads:
+            load.wait()
+        for slot in range(1, parts):
+            for w in sides:
+                weight_copy(slot, w).wait_recv()
+        add_late(0)
+        acts_copy(1).wait_recv()
+        add_late(1)
+        for d in range(1, groups):
+            acts_copy(2 * d).wait_recv()
+            forward(2 * d).start()
+            add_late(2 * d)
+        for d in range(1, groups):
+            forward(2 * d).wait_recv()
+            add_late(2 * d + 1)
+        for k in range(HALVES):
+            total = own[last, k]
+            for i in range(last):
+                to_far(i, k).wait()
+                total = total + far_recv[i, k].astype(jnp.float32)
+            out_ref[:, k * wide : (k + 1) * wide] = total.astype(jnp.bfloat16)
 
     def gather(c, slots):
         pieces = [(own_piece[c], own_stats[c, :, 0:1], own_stats[c, :, 1:2])]
@@ -643,7 +786,7 @@
         def _():
             gather(c, (0, 1))
 
-    ahead, lag = 2, CUTS
+    ahead, lag = 2, CUTS - 1
     for c in range(ahead):
         advance(c)
 
@@ -666,20 +809,21 @@
         def _():
             collect(c - lag)
 
+        @pl.when(c == steps - 2)
+        def _():
+            project_early()
+
         return 0
 
     lax.fori_loop(0, steps, turn, 0)
-    lax.fori_loop(0, here - 1, home, 0)
 
     def rest(c, _):
         collect(c)
         return 0
 
     lax.fori_loop(steps - lag, steps, rest, 0)
-    home(here - 1, 0)
-    load.wait()
-    project(groups, group, core, mate, weight, acts, own, pair_send, pair_recv, far_send,
-            far_recv, pair_sems, far_sems, out_ref)
+    home(early, put_late)
+    project_late()
 
     def drain(c, _):
         side_copy(c).wait_send()
@@ -709,6 +853,13 @@
         return 0
 
     lax.fori_loop(0, steps, drain, 0)
+    for slot in range(1, parts):
+        for w in sides:
+            weight_copy(slot, w).wait_send()
+    acts_copy(1).wait_send()
+    for d in range(1, groups):
+        acts_copy(2 * d).wait_send()
+        forward(2 * d).wait_send()
 
 
 def level_body(parts, q, k, v, dq, dk, dv, routes, weight):
@@ -745,14 +896,19 @@
             pltpu.VMEM((steps, rows, 128), jnp.float32),
             pltpu.VMEM((steps, 2, some, per, 2 * e), half),
             pltpu.VMEM((steps, some, per, 2 * e), half),
-            pltpu.VMEM(weight.shape, half),
-            pltpu.VMEM((2 * tok, heads * e), half),
+            pltpu.VMEM(((heads - 2) * e, weight.shape[1]), half),
+            pltpu.VMEM((parts, 2 * e, width), half),
+            pltpu.VMEM((2 * tok, (heads - 2) * e), half),
+            pltpu.VMEM((parts, 2 * tok, 2 * e), half),
             pltpu.VMEM((groups, HALVES, 2 * tok, width // HALVES), jnp.float32),
             pltpu.VMEM((groups, HALVES, 2 * tok, width // HALVES), half),
             pltpu.VMEM((groups, HALVES, 2 * tok, width // HALVES), half),
             pltpu.VMEM((max(groups - 1, 1), HALVES, 2 * tok, width // HALVES), half),
             pltpu.VMEM((max(groups - 1, 1), HALVES, 2 * tok, width // HALVES), half),
-            dma,
+            dma((heads - 2,)),
+            dma((2,)),
+            dma((2, parts, 2)),
+            dma((2, parts)),
             dma((2, steps)),
             dma((2, steps)),
             dma((2, 2, steps)),
@@ -773,7 +929,7 @@
     n, parts = mesh.shape["seq"], mesh.shape["tensor"]
 
     def run(*args):
-        if n == 2 * LEVELS and args[6].shape[1] % 2 == 0:
+        if n == 2 * LEVELS and args[6].shape[1] % 2 == 0 and args[6].shape[1] >= 4:
             return level_body(parts, *args)
         return body(n, parts, *args)
 

time: 102 us -> 102 us (level); the launches traced: 102 us -> 101 us
  Pallas kernels: 102 us -> 100 us
    pallas_call x1, Pallas kernels: 99.4 us -> 98.2 us  [level_body(): pl.pallas_call(functools.partial(level_kernel, parts), out_shape=shape, i...]
where the time goes in v7:
time: 102 us; the launch traced here: 101 us
  Pallas kernels  100 us (98%)
    pallas_call x1, Pallas kernels, level_body(): pl.pallas_call(functools.partial(level_kernel, parts), out_shape=shape, i...  98.2 us
    pallas_call x1, Pallas kernels, split(): pl.pallas_call(split_kernel, out_shape=(shape, shape), in_specs=[vmem], o...  2.23 us

profile of v7, /device:TPU:16, one launch (start us, length us, event | category | flops | bytes accessed | tf_op | source)
XLA Modules:
  0.0 101.0 jit_solution(11721382966882287583)
XLA Ops:
  0.6 98.2 %shard_map.95.both_ref = bf16[512,1024]{1,0:T(8,128)(2,1)} custom-call(bf16[256,1024]{1,0:T(8,128)(2,1)} %q_ref.1, bf16[256,1024]{1,0:T(8,128)(2,1)} %k_ref.1, bf16[256,1024]{1,0:T(8,128)(2,1)} %v_ref.1, bf16[256,1024]{1,0:T(8,128)(2,1)} %dq_ref.1, bf16[256,1024]{1,0:T(8,128)(2,1)} %dk_ref.1, bf16[256,1024]{1,0:T(8,128)(2,1)} %dv_ref.1, s32[8,256]{1,0:T(8,128)} %bitcast.1, ...), custom_call_target="tpu_custom_call" | custom-call | tf_op jit(solution)/shard_map/pallas_call | solution.py:879
  98.8 2.2 %shard_map.96 = (bf16[256,1024]{1,0:T(8,128)(2,1)}, bf16[256,1024]{1,0:T(8,128)(2,1)}) custom-call(bf16[512,1024]{1,0:T(8,128)(2,1)} %shard_map.95.both_ref), custom_call_target="tpu_custom_call" | custom-call | tf_op jit(solution)/shard_map/pallas_call | solution.py:267

commit v8 on v7

--- a/solution.py
+++ b/solution.py
@@ -562,7 +562,7 @@
             jnp.concatenate([p[1] for p in parts_of], 0),
             jnp.concatenate([p[2] for p in parts_of], 0),
         )
-        stats_out[slot, c] = packed.T[:8]
+        stats_out[slot, c] = packed.T[:2]
         for copy in piece_copies(slot, c, z):
             copy.start()
 
@@ -769,7 +769,7 @@
             for copy in piece_copies(slot, c, 2):
                 copy.wait_recv()
             stats = stats_in[slot, c]
-            stats = jnp.concatenate([stats, jnp.zeros((120, stats.shape[1]), jnp.float32)], 0).T
+            stats = jnp.concatenate([stats, jnp.zeros((126, stats.shape[1]), jnp.float32)], 0).T
             rows = piece_in[slot, c].reshape(some * 2 * per, 2 * e).astype(jnp.float32)
             pieces.append((rows, stats[:, 0:1], stats[:, 1:2]))
         rows = merge(pieces)
@@ -890,8 +890,8 @@
             pltpu.VMEM((2, steps, 2, some, per, 2 * e), half),
             pltpu.VMEM((2, steps, some, 2 * per, 2 * e), half),
             pltpu.VMEM((2, steps, some, 2 * per, 2 * e), half),
-            pltpu.VMEM((2, steps, 8, rows), jnp.float32),
-            pltpu.VMEM((2, steps, 8, rows), jnp.float32),
+            pltpu.VMEM((2, steps, 2, rows), jnp.float32),
+            pltpu.VMEM((2, steps, 2, rows), jnp.float32),
             pltpu.VMEM((steps, rows, 2 * e), jnp.float32),
             pltpu.VMEM((steps, rows, 128), jnp.float32),
             pltpu.VMEM((steps, 2, some, per, 2 * e), half),

time: 102 us -> 101 us (level)
  Pallas kernels: 100 us -> 98.9 us
    pallas_call x1, Pallas kernels: 98.2 us -> 96.7 us  [level_body(): pl.pallas_call(functools.partial(level_kernel, parts), out_shape=shape, i...]
where the time goes in v8:
time: 101 us; the launch traced here: 99.5 us
  Pallas kernels  98.9 us (98%)
    pallas_call x1, Pallas kernels, level_body(): pl.pallas_call(functools.partial(level_kernel, parts), out_shape=shape, i...  96.7 us
    pallas_call x1, Pallas kernels, split(): pl.pallas_call(split_kernel, out_shape=(shape, shape), in_specs=[vmem], o...  2.23 us

profile of v8, /device:TPU:16, one launch (start us, length us, event | category | flops | bytes accessed | tf_op | source)
XLA Modules:
  0.0 99.5 jit_solution(15497771659631799223)
XLA Ops:
  0.6 96.7 %shard_map.95.both_ref = bf16[512,1024]{1,0:T(8,128)(2,1)} custom-call(bf16[256,1024]{1,0:T(8,128)(2,1)} %q_ref.1, bf16[256,1024]{1,0:T(8,128)(2,1)} %k_ref.1, bf16[256,1024]{1,0:T(8,128)(2,1)} %v_ref.1, bf16[256,1024]{1,0:T(8,128)(2,1)} %dq_ref.1, bf16[256,1024]{1,0:T(8,128)(2,1)} %dk_ref.1, bf16[256,1024]{1,0:T(8,128)(2,1)} %dv_ref.1, s32[8,256]{1,0:T(8,128)} %bitcast.1, ...), custom_call_target="tpu_custom_call" | custom-call | tf_op jit(solution)/shard_map/pallas_call | solution.py:879
  97.3 2.2 %shard_map.96 = (bf16[256,1024]{1,0:T(8,128)(2,1)}, bf16[256,1024]{1,0:T(8,128)(2,1)}) custom-call(bf16[512,1024]{1,0:T(8,128)(2,1)} %shard_map.95.both_ref), custom_call_target="tpu_custom_call" | custom-call | tf_op jit(solution)/shard_map/pallas_call | solution.py:267
